TPU v7x, 512 devices: a whole 4x4x16 slice. The times are simulated.
512 devices in a mesh: seq: 16 (over x, z_lo), head: 8 (over z_hi, core), pool: 4 (over y).
Axes of the slice: x: 4, y: 4, z: 16 (z_hi: 4, z_lo: 4; z = z_hi * 4 + z_lo), core: 2. Of those that a mesh axis runs over, the one named last changes fastest.
Arguments:
- mixer_input: bfloat16 [4, 3072, 16384], P('pool', 'seq', 'head'), may hold values from -6 to 6
- gate_input: bfloat16 [4, 3072, 16384], P('pool', 'seq', 'head'), may hold values from -16 to 16
- input_coeff: bfloat16 [4, 3072, 2048], P('pool', 'seq', 'head'), may hold values from -0.375 to 0.375
- output_coeff: bfloat16 [4, 3072, 2048], P('pool', 'seq', 'head'), may hold values from -0.109375 to 0.109375
- log_decay: float32 [4, 256, 3072], P('pool', 'head', 'seq'), may hold values from -2 to 0
- skip_gain: float32 [256], P('head'), may hold values from 0.1 to 1.9
- norm_gain: float32 [16384], P('head'), may hold values from 0.1 to 1.9
- segment_ids: int32 [4, 3072], P('pool', 'seq'), may hold values from 0 to 2, never falling along the last dimension, each value on 1 to 2304 neighbouring positions
- query_rows: bfloat16 [4, 3072, 8192], P('pool', 'seq', 'head'), may hold values from -5 to 5
- key_rows: bfloat16 [4, 3072, 1024], P('pool', 'seq', 'head'), may hold values from -5 to 5
- value_rows: bfloat16 [4, 3072, 1024], P('pool', 'seq', 'head'), may hold values from -6 to 6
- owner_map: int32 [4, 32], P('pool', 'head'), may hold values from 0 to 3, as said below
Outputs:
- mixer_output: bfloat16 [4, 3072, 16384], P('pool', 'seq', 'head')
- attention_out: bfloat16 [4, 3072, 8192], P('pool', 'seq', 'head')
- owned_states: float32 [4, 4, 64, 64, 256], P('pool', None, 'head', 'seq')
- owned_keys: bfloat16 [4, 4, 768, 1024], P('pool', None, 'seq', 'head')
- owned_values: bfloat16 [4, 4, 768, 1024], P('pool', None, 'seq', 'head')
Inputs may be any that keep to these rules, and one draw needn't show every extreme that they name: `owner_map`: for each request and each run of 4 consecutive hand-over groups starting at a multiple of 4, the owners are 0 to 3, each once.
All inputs are finite; a program needn't handle non-finite values.
Results may differ from a plain program's by a relative error of at most 0.0055.
Values may be sent and summed in bfloat16 or wider, within the bound.
A program may use at most 128 MiB of HBM per device.

v0:
```python
import math

import jax
import jax.numpy as jnp
from jax import lax
from jax.sharding import PartitionSpec as P

HEAD_P = 64
STATE = 256
HEAD_DIM = 128


NORM_EPS = 1e-05
HIGH = lax.Precision.HIGHEST
MASK_LOW = -1e30


def entering(part, axis, combine, identity):
    place = lax.axis_index(axis)
    gathered = jax.tree.map(lambda a: lax.all_gather(a, axis), part)
    state = jax.tree.map(lambda a, e: jnp.zeros_like(a) + jnp.asarray(e, a.dtype), part, identity)

    def one(lap, state):
        return combine(
            state, jax.tree.map(lambda a: lax.dynamic_index_in_dim(a, lap, 0, False), gathered)
        )

    return lax.fori_loop(0, place, one, state)


def spread(block, axis, owner):
    block = jnp.where(lax.axis_index(axis) == owner, block, jnp.zeros_like(block))
    return lax.psum(block, axis)


def link_combine(earlier, latter):
    earlier_none = earlier[1][0] < 0.0
    latter_none = latter[1][0] < 0.0
    joined = jnp.where(earlier_none | (latter[0][0] == earlier[1][0]), 1.0, 0.0)
    through = latter[2] * joined
    factor = jnp.where(latter_none, earlier[2], through * earlier[2])
    first_seg = jnp.where(earlier_none, latter[0], earlier[0])
    last_seg = jnp.where(latter_none, earlier[1], latter[1])
    state_sum = jnp.where(latter_none, earlier[3], latter[3] + through[:, None, None] * earlier[3])
    return (first_seg, last_seg, factor, state_sum)


def local(
    mixer_input,
    gate_input,
    input_coeff,
    output_coeff,
    log_decay,
    skip_gain,
    norm_gain,
    segment_ids,
    query_rows,
    key_rows,
    value_rows,
    owner_map,
):
    row_count = mixer_input.shape[1]
    head_count = log_decay.shape[1]
    group_count = input_coeff.shape[2] // STATE
    per_group = head_count // group_count
    seq_index = lax.axis_index("seq")
    seq_count = lax.axis_size("seq")
    pool_count = lax.axis_size("pool")
    seg_ids = segment_ids[0]
    seg_float = seg_ids.astype(jnp.float32)
    x_local = mixer_input[0].reshape(row_count, group_count, per_group, HEAD_P)
    b_local = input_coeff[0].reshape(row_count, group_count, STATE)
    c_local = output_coeff[0].reshape(row_count, group_count, STATE)
    cum = jnp.cumsum(log_decay[0], axis=1)
    places = jnp.arange(row_count)
    same_seg = (seg_ids[:, None] == seg_ids[None, :]) & (places[:, None] >= places[None, :])
    log_gap = cum[:, :, None] - cum[:, None, :]
    decay_mask = jnp.where(same_seg[None], jnp.exp(jnp.where(same_seg[None], log_gap, 0.0)), 0.0)
    inner_prod = jnp.einsum("ign,jgn->gij", c_local, b_local, preferred_element_type=jnp.float32)
    mix_weight = (
        inner_prod[:, None] * decay_mask.reshape(group_count, per_group, row_count, row_count)
    ).astype(jnp.bfloat16)
    intra_part = jnp.einsum(
        "gkij,jgkp->igkp", mix_weight, x_local, preferred_element_type=jnp.float32
    )
    x_wide = x_local.astype(jnp.float32)
    tail_weight = jnp.where((seg_ids == seg_ids[-1])[None, :], jnp.exp(cum[:, -1:] - cum), 0.0)
    tail_x = (x_wide * tail_weight.T.reshape(row_count, group_count, per_group, 1)).astype(
        jnp.bfloat16
    )
    own_state = jnp.einsum(
        "jgkp,jgn->gkpn", tail_x, b_local, preferred_element_type=jnp.float32
    ).reshape(head_count, HEAD_P, STATE)
    own_factor = jnp.exp(cum[:, -1]) * jnp.where(seg_ids[0] == seg_ids[-1], 1.0, 0.0)
    first_seg = seg_float[:1]
    last_seg = seg_float[-1:]
    p_rows = HEAD_P // seq_count
    identity = (
        jnp.full((1,), -1.0, jnp.float32),
        jnp.full((1,), -1.0, jnp.float32),
        jnp.ones((head_count,), jnp.float32),
        jnp.zeros_like(own_state),
    )
    element = (first_seg, last_seg, own_factor, own_state)
    prefix = entering(element, "seq", link_combine, identity)
    prev_last = prefix[1]
    state_in = prefix[3]
    inclusive = link_combine(prefix, element)
    final_all = spread(inclusive[3], "seq", seq_count - 1)
    final_rows = lax.dynamic_slice_in_dim(final_all, seq_index * p_rows, p_rows, 1)
    enter_weight = jnp.where(seg_float[None, :] == prev_last[0], jnp.exp(cum), 0.0)
    carried = jnp.einsum(
        "ign,gkpn->igkp",
        c_local.astype(jnp.float32),
        state_in.reshape(group_count, per_group, HEAD_P, STATE),
        precision=HIGH,
    )
    skip_grid = skip_gain.reshape(group_count, per_group)
    mixed = (
        intra_part
        + carried * enter_weight.T.reshape(row_count, group_count, per_group, 1)
        + skip_grid[None, :, :, None] * x_wide
    )
    mixed = (
        lax.optimization_barrier(mixed.astype(jnp.bfloat16))
        .astype(jnp.float32)
        .reshape(row_count, head_count * HEAD_P)
    )
    gated = mixed * jax.nn.silu(gate_input[0].astype(jnp.float32))
    grouped = gated.reshape(row_count, group_count, per_group * HEAD_P)
    mean_sq = jnp.mean(grouped * grouped, axis=2, keepdims=True)
    normed = (grouped * lax.rsqrt(mean_sq + NORM_EPS)).reshape(row_count, head_count * HEAD_P)
    mixer_output = (normed * norm_gain[None, :]).astype(jnp.bfloat16)[None]
    kv_count = key_rows.shape[2] // HEAD_DIM
    q_groups = query_rows.shape[2] // HEAD_DIM // kv_count
    query_local = query_rows[0].reshape(row_count, kv_count, q_groups, HEAD_DIM)
    score_scale = HEAD_DIM ** (-0.5)
    query_pos = seq_index * row_count + places
    start_carry = (
        jnp.full((kv_count, q_groups, row_count), MASK_LOW, jnp.float32),
        jnp.zeros((kv_count, q_groups, row_count), jnp.float32),
        jnp.zeros((kv_count, q_groups, row_count, HEAD_DIM), jnp.float32),
    )
    seg_wire = seg_ids.astype(jnp.bfloat16)[None]
    key_part = lax.all_gather(key_rows, "seq", axis=1, tiled=True)
    value_part = lax.all_gather(value_rows, "seq", axis=1, tiled=True)
    seg_part = lax.all_gather(seg_wire, "seq", axis=1, tiled=True)
    span_len = key_part.shape[1]
    block_len = math.gcd(span_len, 512)
    block_count = span_len // block_len
    key_blocks = key_part[0].reshape(block_count, block_len, kv_count, HEAD_DIM)
    value_blocks = value_part[0].reshape(block_count, block_len, kv_count, HEAD_DIM)
    seg_blocks = seg_part[0].reshape(block_count, block_len)
    block_starts = jnp.arange(block_count) * block_len

    def visit(running, block):
        run_max, run_sum, run_out = running
        key_blk, value_blk, seg_blk, blk_start = block
        scores = (
            jnp.einsum("ikqd,jkd->kqij", query_local, key_blk, preferred_element_type=jnp.float32)
            * score_scale
        )
        key_pos = blk_start + jnp.arange(block_len)
        seen = (key_pos[None, :] <= query_pos[:, None]) & (
            seg_blk.astype(jnp.float32)[None, :] == seg_float[:, None]
        )
        masked = jnp.where(seen, scores, MASK_LOW)
        new_max = jnp.maximum(run_max, jnp.max(masked, axis=-1))
        rescale = jnp.exp(run_max - new_max)
        expo = jnp.where(seen, jnp.exp(masked - new_max[..., None]), 0.0)
        run_sum = run_sum * rescale + jnp.sum(expo, axis=-1)
        run_out = run_out * rescale[..., None] + jnp.einsum(
            "kqij,jkd->kqid",
            expo.astype(jnp.bfloat16),
            value_blk,
            preferred_element_type=jnp.float32,
        )
        return ((new_max, run_sum, run_out), None)

    result, unused = lax.scan(
        visit, start_carry, (key_blocks, value_blocks, seg_blocks, block_starts)
    )
    run_max, run_sum, run_out = result
    attended = (
        (run_out / run_sum[..., None])
        .transpose(2, 0, 1, 3)
        .reshape(row_count, kv_count * q_groups * HEAD_DIM)
    )
    attention_out = attended.astype(jnp.bfloat16)[None]
    owner_row = owner_map[0]
    slot_ids = jnp.arange(pool_count)
    inverse = jnp.sum(
        jnp.where(owner_row[None, :] == slot_ids[:, None], slot_ids[None, :], 0), axis=1
    )
    group_heads = head_count // pool_count
    state_groups = jnp.take(
        final_rows.reshape(pool_count, group_heads, p_rows, STATE), inverse, axis=0
    )
    owned_states = lax.all_to_all(state_groups, "pool", split_axis=0, concat_axis=0, tiled=True)[
        None
    ]
    page_rows = row_count // pool_count
    key_pages = jnp.take(
        key_rows[0].reshape(pool_count, page_rows, kv_count * HEAD_DIM), inverse, axis=0
    )
    value_pages = jnp.take(
        value_rows[0].reshape(pool_count, page_rows, kv_count * HEAD_DIM), inverse, axis=0
    )
    owned_keys, owned_values = (
        lax.all_to_all(key_pages, "pool", split_axis=0, concat_axis=0, tiled=True),
        lax.all_to_all(value_pages, "pool", split_axis=0, concat_axis=0, tiled=True),
    )
    return (mixer_output, attention_out, owned_states, owned_keys[None], owned_values[None])


def solution(mesh):
    return jax.shard_map(
        local,
        mesh=mesh,
        in_specs=(
            P("pool", "seq", "head"),
            P("pool", "seq", "head"),
            P("pool", "seq", "head"),
            P("pool", "seq", "head"),
            P("pool", "head", "seq"),
            P("head"),
            P("head"),
            P("pool", "seq"),
            P("pool", "seq", "head"),
            P("pool", "seq", "head"),
            P("pool", "seq", "head"),
            P("pool", "head"),
        ),
        out_specs=(
            P("pool", "seq", "head"),
            P("pool", "seq", "head"),
            P("pool", None, "head", "seq", None),
            P("pool", None, "seq", "head"),
            P("pool", None, "seq", "head"),
        ),
        check_vma=False,
    )
```

profile of v0, /device:TPU:6, one launch (start us, length us, event | category | flops | bytes accessed | tf_op | source)
XLA Modules:
  0.0 1046.0 jit_solution(3351215161868687085)
XLA Ops:
  10.1 1.3 compare_reduce_fusion.1
  12.8 1.4 copy.53
  14.8 1.7 fusion.44
  18.6 4.5 all-to-all-start.1
  26.0 1.3 fusion.52
  27.3 42.1 %all-reduce.5 = (f32[16]{0:T(128)S(1)}, f32[512]{0:T(512)S(1)}, f32[16]{0:T(128)S(1)}) all-reduce(f32[16]{0:T(128)S(1)} %get-tuple-element.273, f32[512]{0:T(512)S(1)} %dynamic-update-slice.1, f32[16]{0:T(128)S(1)} %slice_dynamic-update-slice_fusion), channel_id=2, replica_groups=mesh['seq'=16,'head'=8,'pool'=4] {'seq'}, use_global_device_ids=true, to_apply=%add.1 | all-reduce | flops 544 | bytes 4352
  70.4 52.0 %all-reduce.4 = bf16[3072]{0:T(1024)(128)(2,1)S(1)} all-reduce(bf16[3072]{0:T(1024)(128)(2,1)S(1)} %dynamic-update-slice.3), channel_id=1, replica_groups=mesh['seq'=16,'head'=8,'pool'=4] {'seq'}, use_global_device_ids=true, to_apply=%add.4 | all-reduce | flops 3072 | bytes 12288
  126.1 66.1 %all_gather.35 = bf16[1,3072,128]{2,1,0:T(8,128)(2,1)} all-gather(bf16[1,192,128]{2,1,0:T(8,128)(2,1)S(1)} %copy-done.9), channel_id=1, replica_groups=mesh['seq'=16,'head'=8,'pool'=4] {'seq'}, dimensions={1}, use_global_device_ids=true | all-gather | bytes 835584 | tf_op jit(solution)/shard_map/all_gather | solution.py:145
  192.2 62.8 %all_gather.36 = bf16[1,3072,128]{2,1,0:T(8,128)(2,1)} all-gather(bf16[1,192,128]{2,1,0:T(8,128)(2,1)S(1)} %copy-done.10), channel_id=1, replica_groups=mesh['seq'=16,'head'=8,'pool'=4] {'seq'}, dimensions={1}, use_global_device_ids=true | all-gather | bytes 835584 | tf_op jit(solution)/shard_map/all_gather | solution.py:146
  255.0 43.3 %while.31 = (s32[]{:T(128)}, f32[1,8,192]{2,1,0:T(8,128)S(1)}, f32[1,8,192]{2,1,0:T(8,128)S(1)}, f32[1,8,192,128]{3,2,1,0:T(8,128)}, s32[6]{0:T(128)S(1)}, /*ind...) while((s32[]{:T(128)}, f32[1,8,192]{2,1,0:T(8,128)S(1)}, ...), condition=%wide.region_8.9_spmd.clone, body=%wide.region_5.8_spmd.clone.sunk | while | flops 413771968 | bytes 18460136 | solution.py:180
  256.3 1.8 fusion.71
  259.2 2.1 fusion.74
  263.5 1.8 fusion.71
  266.5 2.1 fusion.74
  270.7 1.8 fusion.71
  273.7 2.1 fusion.74
  277.9 1.8 fusion.71
  280.9 2.1 fusion.74
  285.2 1.8 fusion.71
  288.1 2.1 fusion.74
  292.4 1.8 fusion.71
  295.3 2.1 fusion.74
  298.3 1.4 fusion.40
  299.7 449.9 %all-gather.6.cloned.1.call-done = f32[512,64,256]{2,1,0:T(8,128)} async-done(((f32[32,64,256]{2,1,0:T(8,128)}), f32[512,64,256]{2,1,0:T(8,128)}) %all-gather.6.cloned.1.call-update) | async-done | bytes 33554448 | tf_op jit(solution)/shard_map/all_gather | solution.py:20
  749.9 69.8 %while.30 = (s32[]{:T(128)}, f32[1]{0:T(128)}, f32[32,64,256]{2,1,0:T(8,128)S(1)}, s32[]{:T(128)}, f32[16,1]{0,1:T(1,128)S(1)}, /*index=5*/f32[16,32,64,256]{3,2...) while((s32[]{:T(128)}, f32[1]{0:T(128)}, ...), condition=%wide.region_3.4_spmd, body=%wide.region_2.3_spmd.sunk | while | flops 1572907 | bytes 6292100 | solution.py:28
  753.0 2.6 fusion.68
  758.9 2.6 fusion.68
  764.7 2.6 fusion.68
  770.5 2.6 fusion.68
  776.3 2.6 fusion.68
  782.1 2.6 fusion.68
  788.0 2.6 fusion.68
  793.8 2.6 fusion.68
  799.6 2.6 fusion.68
  805.4 2.6 fusion.68
  811.2 2.6 fusion.68
  817.0 2.6 fusion.68
  820.3 3.3 select_select_fusion
  823.6 4.4 all-to-all-start.2
  829.2 1.6 copy.56
  832.0 1.6 all-to-all-done.2
  835.5 2.6 fusion.38
  838.1 1.4 copy.55
  841.0 183.3 %all-reduce.8.cloned.1.call-done = f32[32,64,256]{2,1,0:T(8,128)} async-done(((f32[32,64,256]{2,1,0:T(8,128)}), f32[32,64,256]{2,1,0:T(8,128)}) %all-reduce.8.cloned.1.call-update) | async-done | bytes 2097168 | tf_op jit(solution)/shard_map/psum | solution.py:33
  1026.8 3.7 all-to-all-start
  1030.4 3.1 multiply_convert_fusion.4
  1033.5 2.9 all-to-all-done
  1037.1 1.4 copy.102
  (206 shorter events, 54.6 us)
Async XLA Ops:
  7.2 7.5 copy-start
  7.2 742.4 %all-gather.6.cloned.1.call-start = ((), (), s32[]{:S(2)}) async-start(), calls=%async_computation.4 | async-start | bytes 35651584 | tf_op jit(solution)/shard_map/all_gather | solution.py:20
  14.2 2.3 copy-start.2
  14.7 1.8 copy-start.17
  14.7 1.9 copy-start.10
  14.7 2.5 copy-start.9
  16.5 6.6 copy-start.13
  16.5 106.0 %copy-start.7 = (bf16[1,192,1024]{2,1,0:T(8,128)(2,1)S(1)}, bf16[1,192,1024]{2,1,0:T(8,128)(2,1)}, u32[]{:S(2)}) copy-start(bf16[1,192,1024]{2,1,0:T(8,128)(2,1)} %param.26) | copy-start | bytes 1179652
  16.5 108.7 %copy-start.8 = (bf16[1,192,256]{2,1,0:T(8,128)(2,1)S(1)}, bf16[1,192,256]{2,1,0:T(8,128)(2,1)}, u32[]{:S(2)}) copy-start(bf16[1,192,256]{2,1,0:T(8,128)(2,1)} %param.21) | copy-start | bytes 294916
  17.8 5.2 copy-start.15
  18.6 805.0 %all-to-all-start.1 = ((bf16[4,48,128]{2,1,0:T(8,128)(2,1)}), bf16[4,48,128]{2,1,0:T(8,128)(2,1)}, u32[]{:S(2)}, u32[]{:S(2)}) async-start(bf16[4,48,128]{2,1,0:T(8,128)(2,1)} %get-tuple-element.278), calls=%async_computation.1 | async-start | bytes 98304 | tf_op jit(solution)/shard_map/all_to_all | solution.py:210
  23.0 1001.2 %all-reduce.8.cloned.1.call-start = ((), (), s32[]{:S(2)}) async-start(), calls=%async_computation.3 | async-start | bytes 4194304 | tf_op jit(solution)/shard_map/psum | solution.py:33
  258.1 1.1 copy-start.5
  261.3 0.9 copy-start.6
  265.3 1.1 copy-start.5
  268.5 0.9 copy-start.6
  272.5 1.1 copy-start.5
  275.8 0.9 copy-start.6
  279.7 1.1 copy-start.5
  283.0 0.9 copy-start.6
  287.0 1.1 copy-start.5
  290.2 0.9 copy-start.6
  294.2 1.1 copy-start.5
  297.4 0.9 copy-start.6
  823.5 5.7 copy-start.4
  823.6 10.0 all-to-all-start.2
  834.3 1.2 copy-start.3
  834.3 1.2 copy-start.11
  834.3 1.2 copy-start.12
  834.3 1.2 copy-start.18
  838.1 2.2 copy-start.1
  839.5 186.5 %copy-start.16 = (pred[4]{0:T(512)(128)(4,1)S(1)}, pred[4]{0:T(512)(128)(4,1)}, u32[]{:S(2)}) copy-start(pred[4]{0:T(512)(128)(4,1)} %copy-done.15) | copy-start | bytes 16
  840.2 190.2 %copy-start.14 = (f32[2048]{0:T(1024)S(1)}, f32[2048]{0:T(1024)}, u32[]{:S(2)}) copy-start(f32[2048]{0:T(1024)} %param.24) | copy-start | bytes 24580
  1026.8 9.7 all-to-all-start
Sparse Core Ops, SparseCore 0:
  16.7 732.9 all-gather.5
  823.7 200.5 all-reduce.7
where the time goes:
time: 1050 us
  waiting for transfers between devices  638 us (61%)
  blocking collectives  223 us (21%)
  other arithmetic  65.5 us (6%)
  local copies, waits for them, and re-layouts  34.9 us (3%)
  matrix products  29.6 us (3%)
  loops' own time  24.5 us (2%)
  between operations  18.2 us (2%)
  starting transfers between devices  12.6 us (1%)
    all_gather x1, waiting for transfers between devices, entering(): gathered = jax.tree.map(lambda a: lax.all_gather(a, axis), part)  450 us
    psum x1, waiting for transfers between devices, spread(): return lax.psum(block, axis)  183 us
    unnamed x2, blocking collectives  94.1 us
    all_gather x1, blocking collectives, local(): key_part = lax.all_gather(key_rows, 'seq', axis=1, tiled=True)  66.1 us
    all_gather x1, blocking collectives, local(): value_part = lax.all_gather(value_rows, 'seq', axis=1, tiled=True)  62.8 us
    select_n x12, other arithmetic, link_combine(): jnp.where(latter_none, earlier[3], latter[3] + through[:, None, None] * e...  31.5 us
    another operation x1, loops' own time, entering(): return lax.fori_loop(0, place, one, state)  24 us
  transfers between devices with their start and end apart: 5, of which 4 were waited for; matrix products, arithmetic and copies ran while one was open for 11% of the time, Pallas kernels for 0%

commit v1 on v0

v1 whole, which is shorter than its diff:
```python
import functools
import math

import jax
import jax.numpy as jnp
from jax import lax
from jax.experimental import pallas as pl
from jax.experimental.pallas import tpu as pltpu
from jax.sharding import PartitionSpec as P

HEAD_P = 64
STATE = 256
HEAD_DIM = 128
NORM_EPS = 1e-05
HIGH = lax.Precision.HIGHEST
LOG2E = math.log2(math.e)
FAR = -1e30
F32 = jnp.float32
BF16 = jnp.bfloat16
MESH = pl.DeviceIdType.MESH
NN = (((1,), (0,)), ((), ()))
NT = (((1,), (1,)), ((), ()))


def mm(a, b, dims=NN, precision=None):
    return lax.dot_general(a, b, dims, precision=precision, preferred_element_type=F32)


def expand(parts, grid):
    high = parts.astype(BF16)
    rest = parts - high.astype(F32)
    middle = rest.astype(BF16)
    low = (rest - middle.astype(F32)).astype(BF16)
    return mm(high, grid) + mm(middle, grid) + mm(low, grid)


def kernel(
    n,
    n_pool,
    x_ref,
    z_ref,
    b_ref,
    c_ref,
    ld_ref,
    skip_ref,
    gain_ref,
    seg_ref,
    q_ref,
    k_ref,
    v_ref,
    own_ref,
    mix_out,
    att_out,
    st_out,
    ok_out,
    ov_out,
    s_f32,
    send1,
    recv1,
    send2,
    recv2,
    brief,
    kv,
    qa,
    run_max,
    run_sum,
    run_out,
    mix0,
    enter_x,
    silu_z,
    pages_k,
    pages_v,
    st_rows,
    st_send,
    sem_b,
    sem_1,
    sem_2,
    sem_kz,
    sem_kx,
    sem_pk,
    sem_pv,
    sem_ps,
):
    rows = x_ref.shape[1]
    chans = x_ref.shape[2]
    heads = ld_ref.shape[1]
    q_heads = q_ref.shape[2] // HEAD_DIM
    p_rows = HEAD_P // n
    side = math.isqrt(n)
    groups = n // side
    key_blk = 2 * rows
    blk_per_group = side // 2
    page_rows = rows // n_pool
    grp_heads = heads // n_pool
    me = lax.axis_index("seq")
    my_pool = lax.axis_index("pool")
    grp = me // side
    place = lax.rem(me, side)

    def remote(src, dst, sems, send_at, recv_at, axis, to):
        return pltpu.make_async_remote_copy(
            src_ref=src,
            dst_ref=dst,
            send_sem=sems.at[0, send_at],
            recv_sem=sems.at[1, recv_at],
            device_id={axis: to},
            device_id_type=MESH,
        )

    barrier = pltpu.get_barrier_semaphore()

    def greet(k, u):
        pl.semaphore_signal(
            barrier, inc=1, device_id={"seq": lax.rem(me + k, n)}, device_id_type=MESH
        )
        return u

    lax.fori_loop(1, n, greet, 0)
    for k in range(1, n_pool):
        pl.semaphore_signal(
            barrier, inc=1, device_id={"pool": lax.rem(my_pool + k, n_pool)}, device_id_type=MESH
        )

    row_i = lax.broadcasted_iota(jnp.int32, (rows, rows), 0)
    col_i = lax.broadcasted_iota(jnp.int32, (rows, rows), 1)
    lower = (col_i <= row_i).astype(F32)
    unit = (col_i == row_i).astype(F32)
    ld = ld_ref[0]
    cs = mm(ld, lower, NT, HIGH)
    cs_t = mm(lower, ld, NT, HIGH)
    seg_row = seg_ref[...].astype(F32)
    seg_rows = jnp.broadcast_to(seg_row, (8, rows))
    seg_col = mm(unit, seg_rows, NT)[:, 0:1]
    last_seg = seg_row[:, rows - 1 : rows]

    head_lane = jnp.concatenate(
        [jnp.exp(cs_t[rows - 1 : rows, :]), jnp.zeros((1, 128 - heads), F32)], axis=1
    )
    count_0 = jnp.sum(jnp.where(seg_row == 0.0, 1.0, 0.0), axis=1, keepdims=True)
    count_1 = jnp.sum(jnp.where(seg_row == 1.0, 1.0, 0.0), axis=1, keepdims=True)
    info = [head_lane] + [jnp.broadcast_to(v, (1, 128)) for v in (last_seg, count_0, count_1)]
    brief[me] = jnp.concatenate(info + [jnp.zeros((4, 128), F32)], axis=0)

    mine = pl.multiple_of(me * rows, rows)
    kv[pl.ds(mine, rows), 0:HEAD_DIM] = k_ref[0]
    kv[pl.ds(mine, rows), HEAD_DIM : 2 * HEAD_DIM] = v_ref[0]
    owners = own_ref[...]
    for src, dst in ((k_ref, pages_k), (v_ref, pages_v)):
        for o in range(n_pool):
            page = jnp.zeros((page_rows, HEAD_DIM), F32)
            for g in range(n_pool):
                part = src[0, g * page_rows : (g + 1) * page_rows, :].astype(F32)
                page = jnp.where(owners[:, g : g + 1] == o, part, page)
            dst[o] = page.astype(BF16)

    tail_w = jnp.where(seg_row == last_seg, jnp.exp(cs[:, rows - 1 : rows] - cs), 0.0)
    b_all = b_ref[0]
    for pair in range(heads // 2):
        x_t = x_ref[0, :, pair * 128 : pair * 128 + 128].astype(F32).T
        tail = [
            x_t[i * HEAD_P : (i + 1) * HEAD_P] * tail_w[2 * pair + i : 2 * pair + i + 1]
            for i in range(2)
        ]
        tail_x = jnp.concatenate(tail, axis=0).astype(BF16)
        state = mm(tail_x, b_all)
        for w in range(2):
            s_f32[w, pair * 128 : pair * 128 + 128, :] = state[:, w * 128 : w * 128 + 128]
    for s in range(n):
        for j in range(p_rows):
            for w in range(2):
                part = s_f32[w, pl.ds(s * p_rows + j, heads, stride=HEAD_P), :]
                send1[s, j * heads : (j + 1) * heads, w * 128 : w * 128 + 128] = part.astype(BF16)
    recv1[me] = send1[me]

    pl.semaphore_wait(barrier, n - 1 + n_pool - 1)

    def brief_copy(to, src):
        return remote(brief.at[me], brief.at[src], sem_b, to, src, "seq", to)

    def state_copy(to, src):
        return remote(send1.at[to], recv1.at[src], sem_1, to, src, "seq", to)

    def back_copy(to, src):
        return remote(send2.at[to], recv2.at[src], sem_2, to, src, "seq", to)

    def start_1(k, u):
        to = lax.rem(me + k, n)
        brief_copy(to, me).start()
        state_copy(to, me).start()
        return u

    lax.fori_loop(1, n, start_1, 0)

    def kz_copy(k, src):
        to = grp * side + lax.rem(place + k, side)
        at = pl.ds(pl.multiple_of(src * rows, rows), rows)
        return remote(kv.at[at], kv.at[at], sem_kz, k, k, "seq", to)

    for k in range(1, side):
        kz_copy(k, me).start()

    def pool_copies(k):
        to = lax.rem(my_pool + k, n_pool)
        return (
            remote(pages_k.at[to], ok_out.at[0, my_pool], sem_pk, k, k, "pool", to),
            remote(pages_v.at[to], ov_out.at[0, my_pool], sem_pv, k, k, "pool", to),
        )

    for k in range(1, n_pool):
        for c in pool_copies(k):
            c.start()
    ok_out[0, my_pool] = pages_k[my_pool]
    ov_out[0, my_pool] = pages_v[my_pool]

    head_of = lax.broadcasted_iota(jnp.int32, (heads, chans), 1) // HEAD_P
    grid = (head_of == lax.broadcasted_iota(jnp.int32, (heads, chans), 0)).astype(BF16)
    skip_x = expand(jnp.broadcast_to(skip_ref[...], (8, heads)), grid)[0:1]
    inner = mm(c_ref[0], b_all, NT)
    inner = jnp.where((col_i <= row_i) & (seg_col == seg_row), inner, 0.0)
    half = lax.broadcasted_iota(jnp.int32, (rows, 128), 1) < HEAD_P
    for pair in range(heads // 2):
        lanes = slice(pair * 128, pair * 128 + 128)
        x_pair = x_ref[0, :, lanes]
        y = []
        for h in (2 * pair, 2 * pair + 1):
            gap = jnp.minimum(cs_t[:, h : h + 1] - cs[h : h + 1, :], 0.0)
            y.append(mm((inner * jnp.exp(gap)).astype(BF16), x_pair))
        mix0[:, lanes] = jnp.where(half, y[0], y[1]) + skip_x[:, lanes] * x_pair.astype(F32)
        gate = z_ref[0, :, lanes].astype(F32)
        silu_z[:, lanes] = gate / (1.0 + jnp.exp(-gate))

    lane = lax.broadcasted_iota(jnp.int32, (rows, HEAD_DIM), 1).astype(F32)
    q_doc = jnp.where(lane == seg_col, 1.0, 0.0).astype(BF16)
    for a in range(q_heads):
        qa[a, :, 0:HEAD_DIM] = q_ref[0, :, a * HEAD_DIM : (a + 1) * HEAD_DIM]
        qa[a, :, HEAD_DIM : 2 * HEAD_DIM] = q_doc

    def brief_wait(k, u):
        src = lax.rem(me + k, n)
        brief_copy(src, src).wait_recv()
        return u

    lax.fori_loop(1, n, brief_wait, 0)
    all_brief = brief[...]
    factors = all_brief[:, 0, :]
    lasts = all_brief[:, 1, :]
    before = jnp.concatenate([jnp.full((1, 128), -1.0, F32), lasts[: n - 1]], axis=0)
    through = jnp.where(lasts == before, factors, 0.0)
    pick = lax.broadcasted_iota(jnp.int32, (heads, 128), 0) == lax.broadcasted_iota(
        jnp.int32, (heads, 128), 1
    )
    through_t = mm(pick.astype(F32), through, NT, HIGH)
    edge_0 = jnp.sum(all_brief[:, 2, :], axis=0, keepdims=True)
    edge_1 = edge_0 + jnp.sum(all_brief[:, 3, :], axis=0, keepdims=True)
    prev_last = brief[jnp.maximum(me - 1, 0)][1:2, 0:1]
    prev_last = jnp.where(me == 0, -1.0, prev_last)
    enter = jnp.where(seg_col == prev_last, jnp.exp(cs_t), 0.0)
    enter_x[...] = expand(enter, grid)

    for k in range(1, side):
        kz_copy(k, grp * side + lax.rem(place + side - k, side)).wait_recv()

    def kx_copy(to_grp, src_grp):
        at = pl.ds(pl.multiple_of(src_grp * side * rows, rows), side * rows)
        return remote(kv.at[at], kv.at[at], sem_kx, to_grp, src_grp, "seq", to_grp * side + place)

    for g in range(1, groups):

        @pl.when(grp < g)
        def _():
            kx_copy(g, grp).start()

    scale = HEAD_DIM ** (-0.5) * LOG2E
    blk_row = lax.broadcasted_iota(jnp.int32, (key_blk, HEAD_DIM), 0)
    blk_lane = lax.broadcasted_iota(jnp.int32, (key_blk, HEAD_DIM), 1)
    causal_key = lax.broadcasted_iota(jnp.int32, (rows, key_blk), 1)
    causal_row = lax.broadcasted_iota(jnp.int32, (rows, key_blk), 0)

    def attend(blk, first):
        at = pl.ds(pl.multiple_of(blk * key_blk, key_blk), key_blk)
        key_pos = (blk_row + blk * key_blk).astype(F32)
        doc = jnp.where(key_pos >= edge_0, 1, 0) + jnp.where(key_pos >= edge_1, 1, 0)
        k_doc = jnp.where((doc != blk_lane) & (blk_lane < 3), FAR, 0.0).astype(BF16)
        keys = jnp.concatenate([kv[at, 0:HEAD_DIM], k_doc], axis=1)
        values = kv[at, HEAD_DIM : 2 * HEAD_DIM]
        for a in range(q_heads):
            s = mm(qa[a], keys, NT)
            if first:
                seen = causal_key + blk * key_blk <= causal_row + me * rows
                s = jnp.where(seen, s, FAR)
            top = jnp.max(s, axis=1, keepdims=True)
            if not first:
                old = run_max[a]
                top = jnp.maximum(old[:, 0:1], top)
            e = jnp.exp2((s - top) * scale)
            total = sum(e[:, i : i + 128] for i in range(0, key_blk, 128))
            out = mm(e.astype(BF16), values)
            wide = jnp.broadcast_to(top, (rows, 128))
            if not first:
                shrink = jnp.exp2((old - wide) * scale)
                total = total + run_sum[a] * shrink
                out = out + run_out[a] * shrink
            run_max[a] = wide
            run_sum[a] = total
            run_out[a] = out

    own_blk = me // 2
    grp_blk = grp * blk_per_group
    attend(own_blk, True)

    def attend_own(i, u):
        attend(own_blk - 1 - i, False)
        return u

    lax.fori_loop(0, own_blk - grp_blk, attend_own, 0)

    @pl.when(me == 0)
    def _():
        recv2[...] = jnp.zeros_like(recv2)

    carry = [jnp.zeros((heads, STATE), F32) for _ in range(p_rows)]
    for c in range(n):
        if c > 0:
            for j in range(p_rows):
                send2[c, j * heads : (j + 1) * heads, :] = carry[j].astype(BF16)

            @pl.when(me == c)
            def _():
                recv2[c] = send2[c]

            @pl.when(me != c)
            def _():
                back_copy(c, me).start()

        @pl.when(me != c)
        def _():
            state_copy(c, c).wait_recv()

        keep = through_t[:, c : c + 1]
        for j in range(p_rows):
            part = recv1[c, j * heads : (j + 1) * heads, :].astype(F32)
            carry[j] = part if c == 0 else carry[j] * keep + part

    for o in range(n_pool):
        for j in range(p_rows):
            part = jnp.zeros((grp_heads, STATE), F32)
            for g in range(n_pool):
                given = carry[j][g * grp_heads : (g + 1) * grp_heads]
                part = jnp.where(owners[:, g : g + 1] == o, given, part)
            for w in range(2):
                st_rows[w, pl.ds(j, grp_heads, stride=p_rows), :] = part[:, w * 128 : w * 128 + 128]
        st_send[o] = jnp.concatenate([st_rows[0], st_rows[1]], axis=1)

    def st_copy(k):
        to = lax.rem(my_pool + k, n_pool)
        return remote(st_send.at[to], st_out.at[my_pool], sem_ps, k, k, "pool", to)

    for k in range(1, n_pool):
        st_copy(k).start()
    st_out[my_pool] = st_send[my_pool]

    for g in range(groups - 1):

        @pl.when(grp > g)
        def _():
            kx_copy(g, g).wait_recv()

    def attend_rest(i, u):
        attend(grp_blk - 1 - i, False)
        return u

    lax.fori_loop(0, grp_blk, attend_rest, 0)
    for a in range(q_heads):
        total = jnp.sum(run_sum[a], axis=1, keepdims=True)
        att_out[0, :, a * HEAD_DIM : (a + 1) * HEAD_DIM] = (run_out[a] / total).astype(BF16)

    for s in range(n):

        @pl.when((me > 0) & (me != s))
        def _():
            back_copy(s, s).wait_recv()

        for j in range(p_rows):
            part = recv2[s, j * heads : (j + 1) * heads, :].astype(F32)
            for w in range(2):
                spread = pl.ds(s * p_rows + j, heads, stride=HEAD_P)
                s_f32[w, spread, :] = part[:, w * 128 : w * 128 + 128]
    c_all = c_ref[0]
    square = jnp.zeros((rows, 128), F32)
    for at in range(0, chans, 256):
        lanes = slice(at, at + 256)
        state = jnp.concatenate([s_f32[0, lanes, :], s_f32[1, lanes, :]], axis=1)
        y = mm(c_all, state.astype(BF16), NT)
        mixed = (mix0[:, lanes] + y * enter_x[:, lanes]).astype(BF16).astype(F32)
        gated = mixed * silu_z[:, lanes]
        mix0[:, lanes] = gated
        square = square + gated[:, 0:128] * gated[:, 0:128] + gated[:, 128:] * gated[:, 128:]
    mean = jnp.sum(square, axis=1, keepdims=True) * (1.0 / chans)
    norm = lax.rsqrt(mean + NORM_EPS)
    for at in range(0, chans, 256):
        lanes = slice(at, at + 256)
        mix_out[0, :, lanes] = (mix0[:, lanes] * norm * gain_ref[:, lanes]).astype(BF16)

    def sent(k, u):
        to = lax.rem(me + k, n)
        brief_copy(to, me).wait_send()
        state_copy(to, me).wait_send()

        @pl.when(to > 0)
        def _():
            back_copy(to, me).wait_send()

        return u

    lax.fori_loop(1, n, sent, 0)
    for k in range(1, side):
        kz_copy(k, me).wait_send()
    for g in range(1, groups):

        @pl.when(grp < g)
        def _():
            kx_copy(g, grp).wait_send()

    for k in range(1, n_pool):
        for c in pool_copies(k) + (st_copy(k),):
            c.wait()


def local(n, n_pool, *args):
    (x, z, b, c, ld, skip, gain, seg, q, k, v, owner) = args
    rows, chans = x.shape[1:]
    heads = ld.shape[1]
    q_heads = q.shape[2] // HEAD_DIM
    p_rows = HEAD_P // n
    grp_heads = heads // n_pool
    page_rows = rows // n_pool
    vmem = pl.BlockSpec(memory_space=pltpu.VMEM)
    part = p_rows * heads
    pages = (n_pool, page_rows, HEAD_DIM)
    out = pl.pallas_call(
        functools.partial(kernel, n, n_pool),
        out_shape=(
            jax.ShapeDtypeStruct(x.shape, BF16),
            jax.ShapeDtypeStruct(q.shape, BF16),
            jax.ShapeDtypeStruct((n_pool, grp_heads * p_rows, STATE), F32),
            jax.ShapeDtypeStruct((1,) + pages, BF16),
            jax.ShapeDtypeStruct((1,) + pages, BF16),
        ),
        in_specs=[vmem] * 12,
        out_specs=[vmem] * 5,
        scratch_shapes=[
            pltpu.VMEM((2, chans, STATE // 2), F32),
            pltpu.VMEM((n, part, STATE), BF16),
            pltpu.VMEM((n, part, STATE), BF16),
            pltpu.VMEM((n, part, STATE), BF16),
            pltpu.VMEM((n, part, STATE), BF16),
            pltpu.VMEM((n, 8, 128), F32),
            pltpu.VMEM((n * rows, 2 * HEAD_DIM), BF16),
            pltpu.VMEM((q_heads, rows, 2 * HEAD_DIM), BF16),
            pltpu.VMEM((q_heads, rows, HEAD_DIM), F32),
            pltpu.VMEM((q_heads, rows, HEAD_DIM), F32),
            pltpu.VMEM((q_heads, rows, HEAD_DIM), F32),
            pltpu.VMEM((rows, chans), F32),
            pltpu.VMEM((rows, chans), F32),
            pltpu.VMEM((rows, chans), F32),
            pltpu.VMEM(pages, BF16),
            pltpu.VMEM(pages, BF16),
            pltpu.VMEM((2, grp_heads * p_rows, STATE // 2), F32),
            pltpu.VMEM((n_pool, grp_heads * p_rows, STATE), F32),
            pltpu.SemaphoreType.DMA((2, n)),
            pltpu.SemaphoreType.DMA((2, n)),
            pltpu.SemaphoreType.DMA((2, n)),
            pltpu.SemaphoreType.DMA((2, n)),
            pltpu.SemaphoreType.DMA((2, n)),
            pltpu.SemaphoreType.DMA((2, n)),
            pltpu.SemaphoreType.DMA((2, n)),
            pltpu.SemaphoreType.DMA((2, n)),
        ],
        compiler_params=pltpu.CompilerParams(
            collective_id=0, has_side_effects=True, vmem_limit_bytes=50 * 1024 * 1024
        ),
    )(x, z, b, c, ld, skip.reshape(1, -1), gain.reshape(1, -1), seg, q, k, v, owner)
    mixer, attended, states, keys, values = out
    return mixer, attended, states.reshape(1, n_pool, grp_heads, p_rows, STATE), keys, values


def solution(mesh):
    return jax.shard_map(
        functools.partial(local, mesh.shape["seq"], mesh.shape["pool"]),
        mesh=mesh,
        in_specs=(
            P("pool", "seq", "head"),
            P("pool", "seq", "head"),
            P("pool", "seq", "head"),
            P("pool", "seq", "head"),
            P("pool", "head", "seq"),
            P("head"),
            P("head"),
            P("pool", "seq"),
            P("pool", "seq", "head"),
            P("pool", "seq", "head"),
            P("pool", "seq", "head"),
            P("pool", "head"),
        ),
        out_specs=(
            P("pool", "seq", "head"),
            P("pool", "seq", "head"),
            P("pool", None, "head", "seq", None),
            P("pool", None, "seq", "head"),
            P("pool", None, "seq", "head"),
        ),
        check_vma=False,
    )
```

time: 1050 us -> 107 us (0.10)
  waiting for transfers between devices: 638 us -> 0 us
  blocking collectives: 223 us -> 0 us
  Pallas kernels: 0 us -> 91.6 us
  other arithmetic: 65.5 us -> 0 us
  matrix products: 29.6 us -> 0 us
  loops' own time: 24.5 us -> 0 us
  local copies, waits for them, and re-layouts: 34.9 us -> 12.3 us
  between operations: 18.2 us -> 0.68 us
  starting transfers between devices: 12.6 us -> 0 us
    all_gather x1 -> x0, waiting for transfers between devices: 450 us -> none  [entering(): gathered = jax.tree.map(lambda a: lax.all_gather(a, axis), part)]
    psum x1 -> x0, waiting for transfers between devices: 183 us -> none  [spread(): return lax.psum(block, axis)]
    all_gather x2 -> x0, blocking collectives: 129 us -> none  [the longest x1 66.1 us: local(): key_part = lax.all_gather(key_rows, 'seq', axis=1, tiled=True)]
    unnamed x2 -> x0, blocking collectives: 94.1 us -> none
    pallas_call x0 -> x1, Pallas kernels: none -> 91.6 us  [local(): pl.pallas_call(functools.partial(kernel, n, n_pool), out_shape=(jax.Shape...]
    select_n x17 -> x0, other arithmetic: 36.8 us -> none  [the longest x12 31.5 us: link_combine(): jnp.where(latter_none, earlier[3], latter[3] + through[:, None, None] * e...]
    dot_general x16 -> x0, matrix products: 29.6 us -> none  [the longest x6 12.5 us: visit(): jnp.einsum('kqij,jkd->kqid', expo.astype(jnp.bfloat16), value_blk, prefer...]
    another operation x2 -> x0, loops' own time: 24.5 us -> none  [the longest x1 24 us: entering(): return lax.fori_loop(0, place, one, state)]
  transfers between devices with their start and end apart: 5 -> 0, of which waited for: 4 -> 0; matrix products, arithmetic and copies ran while one was open for 11% -> 0% of each run, Pallas kernels for 0% -> 0%
where the time goes in v1:
time: 107 us; the launch traced here: 105 us
  Pallas kernels  91.6 us (86%)
  local copies, waits for them, and re-layouts  12.3 us (11%)
    pallas_call x1, Pallas kernels, local(): pl.pallas_call(functools.partial(kernel, n, n_pool), out_shape=(jax.Shape...  91.6 us
    unnamed x28, local copies, waits for them, and re-layouts  11.6 us

profile of v1, /device:TPU:6, one launch (start us, length us, event | category | flops | bytes accessed | tf_op | source)
XLA Modules:
  0.0 104.6 jit_solution(11493170266707069350)
XLA Ops:
  0.6 0.0 copy-start.11
  0.6 0.0 copy-start.9
  0.7 0.0 copy-start.10
  0.7 0.6 copy-done.11
  1.3 0.0 copy-done.9
  1.3 0.0 copy-done.10
  1.3 0.0 copy-start
  1.3 1.1 %copy-done = bf16[1,192,2048]{2,1,0:T(8,128)(2,1)S(1)} copy-done((bf16[1,192,2048]{2,1,0:T(8,128)(2,1)S(1)}, bf16[1,192,2048]{2,1,0:T(8,128)(2,1)}, u32[]{:S(2)}) %copy-start) | copy-done | bytes 786456
  2.5 0.0 copy-start.1
  2.5 1.1 %copy-done.1 = bf16[1,192,2048]{2,1,0:T(8,128)(2,1)S(1)} copy-done((bf16[1,192,2048]{2,1,0:T(8,128)(2,1)S(1)}, bf16[1,192,2048]{2,1,0:T(8,128)(2,1)}, u32[]{:S(2)}) %copy-start.1) | copy-done | bytes 786456
  3.6 0.0 copy-start.2
  3.6 1.0 copy-done.2
  4.6 0.0 copy-start.3
  4.6 0.9 copy-done.3
  5.5 0.0 copy-start.4
  5.5 0.9 copy-done.4
  6.4 0.0 copy-start.5
  6.4 0.8 copy-done.5
  7.2 0.0 copy-start.6
  7.2 0.8 copy-done.6
  8.0 0.0 copy-start.7
  8.0 0.8 copy-done.7
  8.7 0.0 copy-start.8
  8.7 0.7 copy-done.8
  9.4 91.6 %shard_map.155 = (bf16[1,192,2048]{2,1,0:T(8,128)(2,1)S(1)}, bf16[1,192,1024]{2,1,0:T(8,128)(2,1)S(1)}, f32[4,32,256]{2,1,0:T(8,128)S(1)}, bf16[1,4,48,128]{3,2,...) custom-call(bf16[1,192,2048]{2,1,0:T(8,128)(2,1)S(1)} %copy-done, bf16[1,192,2048]{2,1,0:T(8,128)(2,1)S(1)} %copy-done.1, ...), custom_call_target="tpu_custom_call" | custom-call | tf_op jit(solution)/shard_map/pallas_call | solution.py:440
  101.0 0.7 reshape.21
  101.7 0.9 copy.21
  102.6 0.7 copy.22
  103.4 0.6 copy.23
  104.0 0.6 copy.24
Async XLA Ops:
  0.6 0.7 copy-start.11
  0.6 0.7 copy-start.9
  0.7 0.7 copy-start.10
  1.3 1.1 %copy-start = (bf16[1,192,2048]{2,1,0:T(8,128)(2,1)S(1)}, bf16[1,192,2048]{2,1,0:T(8,128)(2,1)}, u32[]{:S(2)}) copy-start(bf16[1,192,2048]{2,1,0:T(8,128)(2,1)} %x_ref.1) | copy-start | bytes 2359300
  2.5 1.1 %copy-start.1 = (bf16[1,192,2048]{2,1,0:T(8,128)(2,1)S(1)}, bf16[1,192,2048]{2,1,0:T(8,128)(2,1)}, u32[]{:S(2)}) copy-start(bf16[1,192,2048]{2,1,0:T(8,128)(2,1)} %z_ref.1) | copy-start | bytes 2359300
  3.6 1.0 copy-start.2
  4.6 0.9 copy-start.3
  5.5 0.9 copy-start.4
  6.4 0.8 copy-start.5
  7.2 0.8 copy-start.6
  8.0 0.8 copy-start.7
  8.7 0.7 copy-start.8

commit v2 on v1

v2 whole, which is shorter than its diff:
```python
import functools
import math

import jax
import jax.numpy as jnp
from jax import lax
from jax.experimental import pallas as pl
from jax.experimental.pallas import tpu as pltpu
from jax.sharding import PartitionSpec as P

HEAD_P = 64
STATE = 256
HEAD_DIM = 128
NORM_EPS = 1e-05
HIGH = lax.Precision.HIGHEST
LOG2E = math.log2(math.e)
FAR = -1e30
F32 = jnp.float32
BF16 = jnp.bfloat16
MESH = pl.DeviceIdType.MESH
NN = (((1,), (0,)), ((), ()))
NT = (((1,), (1,)), ((), ()))


def mm(a, b, dims=NN, precision=None):
    return lax.dot_general(a, b, dims, precision=precision, preferred_element_type=F32)


def expand(parts, grid):
    high = parts.astype(BF16)
    rest = parts - high.astype(F32)
    middle = rest.astype(BF16)
    low = (rest - middle.astype(F32)).astype(BF16)
    return mm(high, grid) + mm(middle, grid) + mm(low, grid)


def split_two(parts):
    high = parts.astype(BF16)
    return jnp.concatenate([high, (parts - high.astype(F32)).astype(BF16)], axis=1)


def kernel(
    n,
    n_pool,
    x_hbm,
    z_hbm,
    b_hbm,
    c_hbm,
    ld_hbm,
    skip_hbm,
    gain_hbm,
    seg_hbm,
    q_hbm,
    k_hbm,
    v_hbm,
    own_hbm,
    mix_out,
    att_out,
    st_out,
    ok_out,
    ov_out,
    mix_v,
    att_v,
    x_ref,
    z_ref,
    b_ref,
    c_ref,
    ld_ref,
    skip_ref,
    gain_ref,
    seg_ref,
    own_ref,
    qa,
    kv,
    send1,
    recv1,
    sums,
    others,
    send2,
    recv2,
    brief,
    factor,
    score,
    run_max,
    run_sum,
    run_out,
    mix0,
    enter_x,
    silu_z,
    pages_k,
    pages_v,
    fin,
    fin_t,
    fin_send,
    fin_recv,
    st_send,
    sem_in,
    sem_out,
    sem_b,
    sem_1,
    sem_p,
    sem_2,
    sem_f,
    sem_kz,
    sem_kx,
    sem_pool,
):
    rows = x_hbm.shape[1]
    chans = x_hbm.shape[2]
    heads = ld_hbm.shape[1]
    q_heads = q_hbm.shape[2] // HEAD_DIM
    p_rows = HEAD_P // n
    n_rows = STATE // n
    side = math.isqrt(n)
    groups = n // side
    inner_n = side // 2
    owners_n = groups * inner_n
    span = side * rows
    page_rows = rows // n_pool
    grp_heads = heads // n_pool
    tiles = chans // 128
    me = lax.axis_index("seq")
    my_pool = lax.axis_index("pool")
    grp = me // side
    place = lax.rem(me, side)
    half = place // inner_n
    mine_o = grp * inner_n + lax.rem(place, inner_n)
    mine = pl.multiple_of(me * rows, rows)

    def remote(src, dst, send_sem, recv_sem, axis, to):
        return pltpu.make_async_remote_copy(
            src_ref=src,
            dst_ref=dst,
            send_sem=send_sem,
            recv_sem=recv_sem,
            device_id={axis: to},
            device_id_type=MESH,
        )

    own_rows = pl.ds(mine, rows)
    pairs = [
        (ld_hbm.at[0], ld_ref),
        (seg_hbm, seg_ref),
        (b_hbm.at[0], b_ref),
        (x_hbm.at[0], x_ref),
        (k_hbm.at[0], kv.at[own_rows, pl.ds(0, HEAD_DIM)]),
        (v_hbm.at[0], kv.at[own_rows, pl.ds(HEAD_DIM, HEAD_DIM)]),
        (own_hbm, own_ref),
        (c_hbm.at[0], c_ref),
        (skip_hbm, skip_ref),
        (z_hbm.at[0], z_ref),
        (gain_hbm, gain_ref),
    ] + [
        (
            q_hbm.at[0, :, pl.ds(a * HEAD_DIM, HEAD_DIM)],
            qa.at[pl.ds(a * rows, rows), pl.ds(0, HEAD_DIM)],
        )
        for a in range(q_heads)
    ]
    loads = [pltpu.make_async_copy(s, d, sem_in.at[i]) for i, (s, d) in enumerate(pairs)]
    for load in loads:
        load.start()

    barrier = pltpu.get_barrier_semaphore()

    def greet(k, u):
        pl.semaphore_signal(
            barrier, inc=1, device_id={"seq": lax.rem(me + k, n)}, device_id_type=MESH
        )
        return u

    lax.fori_loop(1, n, greet, 0)
    for k in range(1, n_pool):
        pl.semaphore_signal(
            barrier, inc=1, device_id={"pool": lax.rem(my_pool + k, n_pool)}, device_id_type=MESH
        )

    row_i = lax.broadcasted_iota(jnp.int32, (rows, rows), 0)
    col_i = lax.broadcasted_iota(jnp.int32, (rows, rows), 1)
    lower = (col_i <= row_i).astype(F32)
    unit = (col_i == row_i).astype(F32)
    head_of = lax.broadcasted_iota(jnp.int32, (heads, chans), 1) // HEAD_P
    grid = (head_of == lax.broadcasted_iota(jnp.int32, (heads, chans), 0)).astype(BF16)
    grid_two = jnp.concatenate([grid, grid], axis=0)
    for load in loads[:4]:
        load.wait()
    ld = ld_ref[...]
    cs = mm(ld, lower, NT, HIGH)
    cs_t = mm(lower, ld, NT, HIGH)
    seg_row = seg_ref[...].astype(F32)
    seg_rows = jnp.broadcast_to(seg_row, (8, rows))
    seg_col = mm(unit, seg_rows, NT)[:, 0:1]
    last_seg = seg_row[:, rows - 1 : rows]

    head_lane = jnp.concatenate(
        [jnp.exp(cs_t[rows - 1 : rows, :]), jnp.zeros((1, 128 - heads), F32)], axis=1
    )
    count_0 = jnp.sum(jnp.where(seg_row == 0.0, 1.0, 0.0), axis=1, keepdims=True)
    count_1 = jnp.sum(jnp.where(seg_row == 1.0, 1.0, 0.0), axis=1, keepdims=True)
    info = [head_lane] + [jnp.broadcast_to(v, (1, 128)) for v in (last_seg, count_0, count_1)]
    brief[me] = jnp.concatenate(info + [jnp.zeros((4, 128), F32)], axis=0)

    tail_w = jnp.where(seg_col == last_seg, jnp.exp(cs_t[rows - 1 : rows, :] - cs_t), 0.0)
    tail_two = split_two(tail_w)
    b_t = b_ref[...].astype(F32).T.astype(BF16)
    for at in range(0, chans, 256):
        lanes = slice(at, at + 256)
        tail_x = (x_ref[:, lanes].astype(F32) * mm(tail_two, grid_two[:, lanes])).astype(BF16)
        state = mm(b_t, tail_x).astype(BF16)
        for s in range(n):
            send1[s // 2, s % 2, :, lanes] = state[s * n_rows : (s + 1) * n_rows]

    pl.semaphore_wait(barrier, n - 1 + n_pool - 1)

    def peer(o):
        return (o // inner_n) * side + half * inner_n + lax.rem(o, inner_n)

    def own_copy(k, o, src):
        return remote(
            send1.at[o, k], recv1.at[src, k], sem_1.at[0, k, o], sem_1.at[1, k, src], "seq", peer(o)
        )

    def brief_copy(to, src):
        return remote(
            brief.at[me], brief.at[src], sem_b.at[0, to], sem_b.at[1, src], "seq", to
        )

    def kz_copy(k, src):
        to = grp * side + lax.rem(place + k, side)
        at = pl.ds(pl.multiple_of(src * rows, rows), rows)
        return remote(kv.at[at], kv.at[at], sem_kz.at[0, k], sem_kz.at[1, k], "seq", to)

    for k in range(2):

        def start_own(i, u, k=k):
            own_copy(k, lax.rem(mine_o + i, owners_n), mine_o).start()
            return u

        lax.fori_loop(1, owners_n, start_own, 0)

    def start_brief(i, u):
        brief_copy(lax.rem(me + i, n), me).start()
        return u

    lax.fori_loop(1, n, start_brief, 0)
    for load in loads[4:6]:
        load.wait()
    for k in range(1, side):
        kz_copy(k, me).start()
    for k in range(2):
        recv1[mine_o, k] = send1[mine_o, k]

    loads[6].wait()
    owners = own_ref[...]
    for w, pages in ((0, pages_k), (1, pages_v)):
        for o in range(n_pool):
            page = jnp.zeros((page_rows, HEAD_DIM), F32)
            for g in range(n_pool):
                at = pl.ds(pl.multiple_of(mine + g * page_rows, 16), page_rows)
                part = kv[at, w * HEAD_DIM : (w + 1) * HEAD_DIM].astype(F32)
                page = jnp.where(owners[:, g : g + 1] == o, part, page)
            pages[o] = page.astype(BF16)

    def pool_copy(k, which):
        to = lax.rem(my_pool + k, n_pool)
        src, dst = ((pages_k, ok_out.at[0]), (pages_v, ov_out.at[0]), (st_send, st_out))[which]
        return remote(
            src.at[to],
            dst.at[my_pool],
            sem_pool.at[0, which, k],
            sem_pool.at[1, which, k],
            "pool",
            to,
        )

    for k in range(1, n_pool):
        for which in range(2):
            pool_copy(k, which).start()
    stores = [
        pltpu.make_async_copy(pages_k.at[my_pool], ok_out.at[0, my_pool], sem_out.at[0]),
        pltpu.make_async_copy(pages_v.at[my_pool], ov_out.at[0, my_pool], sem_out.at[1]),
        pltpu.make_async_copy(st_send.at[my_pool], st_out.at[my_pool], sem_out.at[2]),
        pltpu.make_async_copy(att_v, att_out.at[0], sem_out.at[3]),
    ]
    stores[0].start()
    stores[1].start()

    def brief_wait(i, u):
        src = lax.rem(me + i, n)
        brief_copy(src, src).wait_recv()
        return u

    lax.fori_loop(1, n, brief_wait, 0)
    all_brief = brief[...]
    lasts = all_brief[:, 1, :]
    before = jnp.concatenate([jnp.full((1, 128), -1.0, F32), lasts[: n - 1]], axis=0)
    through = jnp.where(lasts == before, all_brief[:, 0, :], 0.0)
    line = [through[c : c + 1] for c in range(n)]
    run = [
        [math.prod(line[g * side + h * inner_n + i] for i in range(inner_n)) for g in range(groups)]
        for h in range(2)
    ]
    table = [jnp.where(half == 0, run[1][max(g - 1, 0)], run[0][g]) for g in range(groups)]
    for g in range(groups):
        for i in range(inner_n):
            a, b = line[g * side + i], line[g * side + inner_n + i]
            table.append(jnp.where(half == 0, a, b))
    table.append(run[1][groups - 1])
    end_at = len(table) - 1
    table = jnp.concatenate(table + [jnp.zeros((16 - len(table), 128), F32)], axis=0)
    factor[...] = expand(table[:, 0:heads], grid)
    edge_0 = jnp.sum(all_brief[:, 2, :], axis=0, keepdims=True)
    edge_1 = edge_0 + jnp.sum(all_brief[:, 3, :], axis=0, keepdims=True)
    prev_last = brief[jnp.maximum(me - 1, 0)][1:2, 0:1]
    prev_last = jnp.where(me == 0, -1.0, prev_last)
    enter_two = split_two(jnp.where(seg_col == prev_last, jnp.exp(cs_t), 0.0))

    for load in loads[7:]:
        load.wait()
    skip_x = expand(jnp.broadcast_to(skip_ref[...], (8, heads)), grid)[0:1]
    inner = mm(c_ref[...], b_t)
    inner = jnp.where((col_i <= row_i) & (seg_col == seg_row), inner, 0.0)
    first_half = lax.broadcasted_iota(jnp.int32, (rows, 128), 1) < HEAD_P

    def within(pair):
        lanes = slice(pair * 128, pair * 128 + 128)
        x_pair = x_ref[:, lanes]
        y = []
        for h in (2 * pair, 2 * pair + 1):
            gap = jnp.minimum(cs_t[:, h : h + 1] - cs[h : h + 1, :], 0.0)
            y.append(mm((inner * jnp.exp(gap)).astype(BF16), x_pair))
        mix0[:, lanes] = jnp.where(first_half, y[0], y[1]) + skip_x[:, lanes] * x_pair.astype(F32)
        gate = z_ref[:, lanes].astype(F32)
        silu_z[:, lanes] = gate / (1.0 + jnp.exp(-gate))
        enter_x[:, lanes] = mm(enter_two, grid_two[:, lanes])

    for pair in range(heads // 2):
        within(pair)

    def sum_copy(k):
        to = grp * side + (1 - half) * inner_n + lax.rem(place, inner_n)
        return remote(
            sums.at[k],
            others.at[k, pl.ds(1, groups)],
            sem_p.at[0, k],
            sem_p.at[1, k],
            "seq",
            to,
        )

    for k in range(2):

        def wait_own(i, u, k=k):
            o = lax.rem(mine_o + i, owners_n)
            own_copy(k, o, o).wait_recv()
            return u

        lax.fori_loop(1, owners_n, wait_own, 0)
        for g in range(groups):
            total = recv1[g * inner_n, k].astype(F32)
            for i in range(1, inner_n):
                at = groups + g * inner_n + i
                total = total * factor[at : at + 1, :] + recv1[g * inner_n + i, k].astype(F32)
            sums[k, g] = total.astype(BF16)
        sum_copy(k).start()

    lane = lax.broadcasted_iota(jnp.int32, (rows, HEAD_DIM), 1).astype(F32)
    q_doc = jnp.where(lane == seg_col, 1.0, 0.0).astype(BF16)
    for a in range(q_heads):
        qa[a * rows : (a + 1) * rows, HEAD_DIM : 2 * HEAD_DIM] = q_doc

    for k in range(1, side):
        kz_copy(k, grp * side + lax.rem(place + side - k, side)).wait_recv()

    def kx_copy(to_grp, src_grp):
        at = pl.ds(pl.multiple_of(src_grp * span, span), span)
        to = to_grp * side + place
        return remote(
            kv.at[at], kv.at[at], sem_kx.at[0, to_grp], sem_kx.at[1, src_grp], "seq", to
        )

    for g in range(1, groups):

        @pl.when(grp < g)
        def _():
            kx_copy(g, grp).start()

    scale = HEAD_DIM ** (-0.5) * LOG2E
    key_lane = lax.broadcasted_iota(jnp.int32, (HEAD_DIM, span), 1)
    doc_row = lax.broadcasted_iota(jnp.int32, (HEAD_DIM, span), 0)
    causal_key = lax.broadcasted_iota(jnp.int32, (rows, span), 1)
    causal_row = lax.broadcasted_iota(jnp.int32, (rows, span), 0)
    edges = [jnp.concatenate([e] * (span // 128), axis=1) for e in (edge_0, edge_1)]

    def attend(g, first):
        at = pl.ds(pl.multiple_of(g * span, span), span)
        key_pos = (key_lane + g * span).astype(F32)
        doc = jnp.where(key_pos >= edges[0], 1, 0) + jnp.where(key_pos >= edges[1], 1, 0)
        k_doc = jnp.where((doc != doc_row) & (doc_row < 3), FAR, 0.0).astype(BF16)
        k_t = kv[at, 0:HEAD_DIM].astype(F32).T.astype(BF16)
        keys = jnp.concatenate([k_t, k_doc], axis=0)
        for a in range(q_heads):
            own = slice(a * rows, (a + 1) * rows)
            s = mm(qa[own, :], keys)
            if first:
                s = jnp.where(causal_key + g * span <= causal_row + me * rows, s, FAR)
            score[own, :] = s
            top = functools.reduce(jnp.maximum, [s[:, i : i + 128] for i in range(0, span, 128)])
            if not first:
                top = jnp.maximum(top, run_max[own])
            top = jnp.broadcast_to(jnp.max(top, axis=1, keepdims=True), (rows, 128))
            if not first:
                shrink = jnp.exp2((run_max[own] - top) * scale)
                run_sum[own] = run_sum[own] * shrink
                run_out[own] = run_out[own] * shrink
            run_max[own] = top
        values = kv[at, HEAD_DIM : 2 * HEAD_DIM]
        for a in range(q_heads):
            own = slice(a * rows, (a + 1) * rows)
            top = run_max[own]
            total = None if first else run_sum[own]
            weights = []
            for i in range(0, span, 128):
                e = jnp.exp2((score[own, i : i + 128] - top) * scale)
                total = e if total is None else total + e
                weights.append(e.astype(BF16))
            out = mm(jnp.concatenate(weights, axis=1), values)
            run_sum[own] = total
            run_out[own] = out if first else run_out[own] + out

    attend(grp, True)

    others[:, 0] = jnp.zeros_like(others[:, 0])

    def back_copy(k, o, src):
        return remote(
            send2.at[o, k], recv2.at[src, k], sem_2.at[0, k, o], sem_2.at[1, k, src], "seq", peer(o)
        )

    for k in range(2):
        sum_copy(k).wait_recv()
        carry = jnp.zeros((n_rows, chans), F32)
        for g in range(groups):
            carry = carry * factor[g : g + 1, :] + others[k, g + half].astype(F32)
            for i in range(inner_n):
                o = g * inner_n + i
                send2[o, k] = carry.astype(BF16)
                at = groups + o
                carry = carry * factor[at : at + 1, :] + recv1[o, k].astype(F32)

        def start_back(i, u, k=k):
            back_copy(k, lax.rem(mine_o + i, owners_n), mine_o).start()
            return u

        lax.fori_loop(1, owners_n, start_back, 0)
        recv2[mine_o, k] = send2[mine_o, k]

        @pl.when(half == k)
        def _():
            if k == 0:
                last = factor[end_at : end_at + 1, :]
                fin[...] = carry * last + others[k, groups].astype(F32)
            else:
                fin[...] = carry

    block_at = 2 * mine_o + half
    stacked = jnp.concatenate([fin[:, t * 128 : (t + 1) * 128] for t in range(tiles)], axis=0)
    fin_t[...] = stacked.T
    for s in range(n):
        for w in range(2):
            at = w * HEAD_P + s * p_rows
            fin_send[s, w * p_rows : (w + 1) * p_rows, :] = fin_t[at : at + p_rows, :]

    def fin_copy(to, src_block):
        return remote(
            fin_send.at[to],
            fin_recv.at[src_block],
            sem_f.at[0, to],
            sem_f.at[1, src_block],
            "seq",
            to,
        )

    def start_fin(i, u):
        fin_copy(lax.rem(me + i, n), block_at).start()
        return u

    lax.fori_loop(1, n, start_fin, 0)
    fin_recv[block_at] = fin_send[me]

    for g in range(groups - 1):

        @pl.when(grp > g)
        def _():
            kx_copy(g, g).wait_recv()

    def attend_rest(i, u):
        attend(grp - 1 - i, False)
        return u

    lax.fori_loop(0, grp, attend_rest, 0)
    for a in range(q_heads):
        own = slice(a * rows, (a + 1) * rows)
        total = jnp.sum(run_sum[own], axis=1, keepdims=True)
        att_v[:, a * HEAD_DIM : (a + 1) * HEAD_DIM] = (run_out[own] / total).astype(BF16)
    stores[3].start()

    def wait_fin(i, u):
        src = lax.rem(block_at + i, n)
        fin_copy(me, src).wait_recv()
        return u

    lax.fori_loop(1, n, wait_fin, 0)
    last = [
        jnp.concatenate(
            [fin_recv[s, :, t * n_rows : (t + 1) * n_rows] for s in range(n)], axis=1
        )
        for t in range(tiles)
    ]
    per = tiles // n_pool
    for o in range(n_pool):
        for t in range(per):
            part = jnp.zeros_like(last[0])
            for g in range(n_pool):
                part = jnp.where(owners[:, g : g + 1] == o, last[g * per + t], part)
            for w in range(2):
                st_send[o, 2 * t + w] = part[w * p_rows : (w + 1) * p_rows]
    for k in range(1, n_pool):
        pool_copy(k, 2).start()
    stores[2].start()

    for k in range(2):

        def sent(i, u, k=k):
            o = lax.rem(mine_o + i, owners_n)
            own_copy(k, o, mine_o).wait_send()
            back_copy(k, o, mine_o).wait_send()
            return u

        lax.fori_loop(1, owners_n, sent, 0)
        sum_copy(k).wait_send()

    def sent_all(i, u):
        to = lax.rem(me + i, n)
        brief_copy(to, me).wait_send()
        fin_copy(to, block_at).wait_send()
        return u

    lax.fori_loop(1, n, sent_all, 0)
    for k in range(1, side):
        kz_copy(k, me).wait_send()
    for g in range(1, groups):

        @pl.when(grp < g)
        def _():
            kx_copy(g, grp).wait_send()

    for k in range(1, n_pool):
        for which in range(2):
            pool_copy(k, which).wait()

    for k in range(2):

        def wait_back(i, u, k=k):
            o = lax.rem(mine_o + i, owners_n)
            back_copy(k, o, o).wait_recv()
            return u

        lax.fori_loop(1, owners_n, wait_back, 0)
    c_all = c_ref[...]
    square = jnp.zeros((rows, 128), F32)
    for at in range(0, chans, 256):
        lanes = slice(at, at + 256)
        entered = jnp.concatenate([recv2[s // 2, s % 2, :, lanes] for s in range(n)], axis=0)
        y = mm(c_all, entered)
        mixed = (mix0[:, lanes] + y * enter_x[:, lanes]).astype(BF16).astype(F32)
        gated = mixed * silu_z[:, lanes]
        mix0[:, lanes] = gated
        square = square + gated[:, 0:128] * gated[:, 0:128] + gated[:, 128:] * gated[:, 128:]
    mean = jnp.sum(square, axis=1, keepdims=True) * (1.0 / chans)
    norm = lax.rsqrt(mean + NORM_EPS)
    part = chans // 4
    for at in range(0, chans, 256):
        lanes = slice(at, at + 256)
        mix_v[:, lanes] = (mix0[:, lanes] * norm * gain_ref[:, lanes]).astype(BF16)
        if (at + 256) % part == 0:
            done = pl.ds(at + 256 - part, part)
            store = pltpu.make_async_copy(
                mix_v.at[:, done], mix_out.at[0, :, done], sem_out.at[4 + at // part]
            )
            store.start()
            stores.append(store)
    for k in range(1, n_pool):
        pool_copy(k, 2).wait()
    for store in stores:
        store.wait()


def store(*refs):
    count = (len(refs) - 1) // 2
    sem = refs[-1]
    copies = [
        pltpu.make_async_copy(refs[i], refs[count + i], sem.at[i]) for i in range(count)
    ]
    for copy in copies:
        copy.start()
    for copy in copies:
        copy.wait()


def local(n, n_pool, *args):
    (x, z, b, c, ld, skip, gain, seg, q, k, v, owner) = args
    rows, chans = x.shape[1:]
    heads = ld.shape[1]
    q_heads = q.shape[2] // HEAD_DIM
    p_rows = HEAD_P // n
    n_rows = STATE // n
    side = math.isqrt(n)
    groups = n // side
    owners_n = n // 2
    grp_heads = heads // n_pool
    page_rows = rows // n_pool
    tiles = chans // 128
    hbm = pl.BlockSpec(memory_space=pltpu.HBM)
    pages = (n_pool, page_rows, HEAD_DIM)
    states = (n_pool, grp_heads, p_rows, STATE)
    part = (owners_n, 2, n_rows, chans)
    dma = pltpu.SemaphoreType.DMA
    out = pl.pallas_call(
        functools.partial(kernel, n, n_pool),
        out_shape=(
            jax.ShapeDtypeStruct(x.shape, BF16),
            jax.ShapeDtypeStruct(q.shape, BF16),
            jax.ShapeDtypeStruct(states, F32),
            jax.ShapeDtypeStruct((1,) + pages, BF16),
            jax.ShapeDtypeStruct((1,) + pages, BF16),
        ),
        in_specs=[hbm] * 12,
        out_specs=[hbm] * 5,
        scratch_shapes=[
            pltpu.VMEM((rows, chans), BF16),
            pltpu.VMEM((rows, q_heads * HEAD_DIM), BF16),
            pltpu.VMEM((rows, chans), BF16),
            pltpu.VMEM((rows, chans), BF16),
            pltpu.VMEM((rows, STATE), BF16),
            pltpu.VMEM((rows, STATE), BF16),
            pltpu.VMEM((heads, rows), F32),
            pltpu.VMEM((1, heads), F32),
            pltpu.VMEM((1, chans), F32),
            pltpu.VMEM((1, rows), jnp.int32),
            pltpu.VMEM((1, n_pool), jnp.int32),
            pltpu.VMEM((q_heads * rows, 2 * HEAD_DIM), BF16),
            pltpu.VMEM((n * rows, 2 * HEAD_DIM), BF16),
            pltpu.VMEM(part, BF16),
            pltpu.VMEM(part, BF16),
            pltpu.VMEM((2, groups, n_rows, chans), BF16),
            pltpu.VMEM((2, groups + 1, n_rows, chans), BF16),
            pltpu.VMEM(part, BF16),
            pltpu.VMEM(part, BF16),
            pltpu.VMEM((n, 8, 128), F32),
            pltpu.VMEM((16, chans), F32),
            pltpu.VMEM((q_heads * rows, side * rows), F32),
            pltpu.VMEM((q_heads * rows, 128), F32),
            pltpu.VMEM((q_heads * rows, 128), F32),
            pltpu.VMEM((q_heads * rows, HEAD_DIM), F32),
            pltpu.VMEM((rows, chans), F32),
            pltpu.VMEM((rows, chans), F32),
            pltpu.VMEM((rows, chans), F32),
            pltpu.VMEM(pages, BF16),
            pltpu.VMEM(pages, BF16),
            pltpu.VMEM((n_rows, chans), F32),
            pltpu.VMEM((128, tiles * n_rows), F32),
            pltpu.VMEM((n, 2 * p_rows, tiles * n_rows), F32),
            pltpu.VMEM((n, 2 * p_rows, tiles * n_rows), F32),
            pltpu.VMEM(states, F32),
            dma((11 + q_heads,)),
            dma((8,)),
            dma((2, n)),
            dma((2, 2, owners_n)),
            dma((2, 2)),
            dma((2, 2, owners_n)),
            dma((2, n)),
            dma((2, side)),
            dma((2, groups)),
            dma((2, 3, n_pool)),
        ],
        compiler_params=pltpu.CompilerParams(
            collective_id=0, has_side_effects=True, vmem_limit_bytes=60 * 1024 * 1024
        ),
    )(x, z, b, c, ld, skip.reshape(1, -1), gain.reshape(1, -1), seg, q, k, v, owner)
    out = pl.pallas_call(
        store,
        out_shape=tuple(jax.ShapeDtypeStruct(o.shape, o.dtype) for o in out),
        in_specs=[hbm] * 5,
        out_specs=[hbm] * 5,
        scratch_shapes=[dma((5,))],
        compiler_params=pltpu.CompilerParams(vmem_limit_bytes=60 * 1024 * 1024),
    )(*out)
    mixer, attended, owned, keys, values = out
    return mixer, attended, owned[None], keys, values


def solution(mesh):
    return jax.shard_map(
        functools.partial(local, mesh.shape["seq"], mesh.shape["pool"]),
        mesh=mesh,
        in_specs=(
            P("pool", "seq", "head"),
            P("pool", "seq", "head"),
            P("pool", "seq", "head"),
            P("pool", "seq", "head"),
            P("pool", "head", "seq"),
            P("head"),
            P("head"),
            P("pool", "seq"),
            P("pool", "seq", "head"),
            P("pool", "seq", "head"),
            P("pool", "seq", "head"),
            P("pool", "head"),
        ),
        out_specs=(
            P("pool", "seq", "head"),
            P("pool", "seq", "head"),
            P("pool", None, "head", "seq", None),
            P("pool", None, "seq", "head"),
            P("pool", None, "seq", "head"),
        ),
        check_vma=False,
    )
```

time: 107 us -> 115 us (1.075); the launches traced: 105 us -> 114 us
  Pallas kernels: 91.6 us -> 114 us
  local copies, waits for them, and re-layouts: 12.3 us -> 0 us
    pallas_call x0 -> x1, Pallas kernels: none -> 43.8 us  [local(): pl.pallas_call(store, out_shape=tuple((jax.ShapeDtypeStruct(o.shape, o.dt...]
    pallas_call x1, Pallas kernels: 91.6 us -> 69.9 us  [local(): pl.pallas_call(functools.partial(kernel, n, n_pool), out_shape=(jax.Shape...]
    unnamed x28 -> x0, local copies, waits for them, and re-layouts: 11.6 us -> none
where the time goes in v2:
time: 115 us; the launch traced here: 114 us
  Pallas kernels  114 us (99%)
    pallas_call x1, Pallas kernels, local(): pl.pallas_call(functools.partial(kernel, n, n_pool), out_shape=(jax.Shape...  69.9 us
    pallas_call x1, Pallas kernels, local(): pl.pallas_call(store, out_shape=tuple((jax.ShapeDtypeStruct(o.shape, o.dt...  43.8 us

profile of v2, /device:TPU:6, one launch (start us, length us, event | category | flops | bytes accessed | tf_op | source)
XLA Modules:
  0.0 114.4 jit_solution(9588066191794075448)
XLA Ops:
  0.6 69.9 %shard_map.155 = (bf16[1,192,2048]{2,1,0:T(8,128)(2,1)}, bf16[1,192,1024]{2,1,0:T(8,128)(2,1)}, f32[4,8,4,256]{3,2,1,0:T(4,128)}, bf16[1,4,48,128]{3,2,1,0:T(8,128)(2,1)}, bf16[1,4,48,128]{3,2,1,0:T(8,128)(2,1)}) custom-call(bf16[1,192,2048]{2,1,0:T(8,128)(2,1)} %x_hbm.1, bf16[1,192,2048]{2,1,0:T(8,128)(2,1)} %z_hbm.1, bf16[1,192,256]{2,1,0:T(8,128)(2,1)} %b_hbm.1, ...), custom_call_target="tpu_custom_call" | custom-call | tf_op jit(solution)/shard_map/pallas_call | solution.py:629
  70.6 43.8 %shard_map.156 = (bf16[1,192,2048]{2,1,0:T(8,128)(2,1)}, bf16[1,192,1024]{2,1,0:T(8,128)(2,1)}, f32[4,8,4,256]{3,2,1,0:T(4,128)}, bf16[1,4,48,128]{3,2,1,0:T(8,128)(2,1)}, bf16[1,4,48,128]{3,2,1,0:T(8,128)(2,1)}) custom-call(bf16[1,192,2048]{2,1,0:T(8,128)(2,1)} %get-tuple-element.15.refs_0_, bf16[1,192,1024]{2,1,0:T(8,128)(2,1)} %get-tuple-element.16.refs_1_, ...), custom_call_target="tpu_custom_call" | custom-call | tf_op jit(solution)/shard_map/pallas_call | solution.py:691

commit v3 on v2

v3 whole, which is shorter than its diff:
```python
import functools
import math

import jax
import jax.numpy as jnp
from jax import lax
from jax.experimental import pallas as pl
from jax.experimental.pallas import tpu as pltpu
from jax.sharding import PartitionSpec as P

HEAD_P = 64
STATE = 256
HEAD_DIM = 128
NORM_EPS = 1e-05
HIGH = lax.Precision.HIGHEST
LOG2E = math.log2(math.e)
FAR = -1e30
F32 = jnp.float32
BF16 = jnp.bfloat16
MESH = pl.DeviceIdType.MESH
NN = (((1,), (0,)), ((), ()))
NT = (((1,), (1,)), ((), ()))


def mm(a, b, dims=NN, precision=None):
    return lax.dot_general(a, b, dims, precision=precision, preferred_element_type=F32)


def expand(parts, grid):
    high = parts.astype(BF16)
    rest = parts - high.astype(F32)
    middle = rest.astype(BF16)
    low = (rest - middle.astype(F32)).astype(BF16)
    return mm(high, grid) + mm(middle, grid) + mm(low, grid)


def split_two(parts):
    high = parts.astype(BF16)
    return jnp.concatenate([high, (parts - high.astype(F32)).astype(BF16)], axis=1)


def kernel(
    n,
    n_pool,
    x_hbm,
    z_hbm,
    b_hbm,
    c_hbm,
    ld_hbm,
    skip_hbm,
    gain_hbm,
    seg_hbm,
    q_hbm,
    k_hbm,
    v_hbm,
    own_hbm,
    mix_out,
    att_out,
    st_out,
    ok_out,
    ov_out,
    mix_v,
    att_v,
    x_ref,
    z_ref,
    b_ref,
    c_ref,
    ld_ref,
    skip_ref,
    gain_ref,
    seg_ref,
    own_ref,
    qa,
    kv,
    send1,
    recv1,
    sums,
    others,
    send2,
    recv2,
    brief,
    factor,
    score,
    run_max,
    run_sum,
    run_out,
    mix0,
    enter_x,
    silu_z,
    pages,
    fin_t,
    fin_send,
    fin_recv,
    st_send,
    sem_in,
    sem_out,
    sem_b,
    sem_1,
    sem_p,
    sem_2,
    sem_f,
    sem_kz,
    sem_kx,
    sem_pool,
):
    rows = x_hbm.shape[1]
    chans = x_hbm.shape[2]
    heads = ld_hbm.shape[1]
    q_heads = q_hbm.shape[2] // HEAD_DIM
    p_rows = HEAD_P // n
    n_rows = STATE // n
    side = math.isqrt(n)
    groups = n // side
    inner_n = side // 2
    owners_n = groups * inner_n
    half_chans = chans // 2
    chunks = 4
    span = side * rows
    page_rows = rows // n_pool
    grp_heads = heads // n_pool
    tiles = chans // 128
    me = lax.axis_index("seq")
    my_pool = lax.axis_index("pool")
    grp = me // side
    place = lax.rem(me, side)
    half = place // inner_n
    mine_o = grp * inner_n + lax.rem(place, inner_n)
    mine = pl.multiple_of(me * rows, rows)

    def remote(src, dst, send_sem, recv_sem, axis, to):
        return pltpu.make_async_remote_copy(
            src_ref=src,
            dst_ref=dst,
            send_sem=send_sem,
            recv_sem=recv_sem,
            device_id={axis: to},
            device_id_type=MESH,
        )

    own_rows = pl.ds(mine, rows)
    pairs = [
        (ld_hbm.at[0], ld_ref),
        (seg_hbm, seg_ref),
        (k_hbm.at[0], kv.at[own_rows, pl.ds(0, HEAD_DIM)]),
        (v_hbm.at[0], kv.at[own_rows, pl.ds(HEAD_DIM, HEAD_DIM)]),
        (b_hbm.at[0], b_ref),
        (x_hbm.at[0], x_ref),
        (own_hbm, own_ref),
        (c_hbm.at[0], c_ref),
        (skip_hbm, skip_ref),
        (z_hbm.at[0], z_ref),
        (gain_hbm, gain_ref),
    ] + [
        (
            q_hbm.at[0, :, pl.ds(a * HEAD_DIM, HEAD_DIM)],
            qa.at[pl.ds(a * rows, rows), pl.ds(0, HEAD_DIM)],
        )
        for a in range(q_heads)
    ]
    loads = [pltpu.make_async_copy(s, d, sem_in.at[i]) for i, (s, d) in enumerate(pairs)]
    for load in loads:
        load.start()

    barrier = pltpu.get_barrier_semaphore()

    for k in range(1, n):
        pl.semaphore_signal(
            barrier, inc=1, device_id={"seq": lax.rem(me + k, n)}, device_id_type=MESH
        )
    for k in range(1, n_pool):
        pl.semaphore_signal(
            barrier, inc=1, device_id={"pool": lax.rem(my_pool + k, n_pool)}, device_id_type=MESH
        )

    row_i = lax.broadcasted_iota(jnp.int32, (rows, rows), 0)
    col_i = lax.broadcasted_iota(jnp.int32, (rows, rows), 1)
    lower = (col_i <= row_i).astype(F32)
    unit = (col_i == row_i).astype(F32)
    head_of = lax.broadcasted_iota(jnp.int32, (heads, chans), 1) // HEAD_P
    grid = (head_of == lax.broadcasted_iota(jnp.int32, (heads, chans), 0)).astype(BF16)
    grid_two = jnp.concatenate([grid, grid], axis=0)
    for load in loads[:2]:
        load.wait()
    ld = ld_ref[...]
    cs = mm(ld, lower, NT, HIGH)
    cs_t = mm(lower, ld, NT, HIGH)
    seg_row = seg_ref[...].astype(F32)
    seg_rows = jnp.broadcast_to(seg_row, (8, rows))
    seg_col = mm(unit, seg_rows, NT)[:, 0:1]
    last_seg = seg_row[:, rows - 1 : rows]

    head_lane = jnp.concatenate(
        [jnp.exp(cs_t[rows - 1 : rows, :]), jnp.zeros((1, 128 - heads), F32)], axis=1
    )
    count_0 = jnp.sum(jnp.where(seg_row == 0.0, 1.0, 0.0), axis=1, keepdims=True)
    count_1 = jnp.sum(jnp.where(seg_row == 1.0, 1.0, 0.0), axis=1, keepdims=True)
    info = [head_lane] + [jnp.broadcast_to(v, (1, 128)) for v in (last_seg, count_0, count_1)]
    brief[half, mine_o] = jnp.concatenate(info + [jnp.zeros((4, 128), F32)], axis=0)

    pl.semaphore_wait(barrier, n - 1 + n_pool - 1)

    def peer(o):
        return (o // inner_n) * side + half * inner_n + lax.rem(o, inner_n)

    across = grp * side + (1 - half) * inner_n + lax.rem(place, inner_n)

    peers = []
    for i in range(1, owners_n):
        o = lax.rem(mine_o + i, owners_n)
        peers.append((o, peer(o)))

    def each_peer(act):
        for p in peers:
            act(p)

    def own_copy(k, p):
        return remote(
            send1.at[k, p[0]], recv1.at[k, mine_o], sem_1.at[0, k], sem_1.at[1, k], "seq", p[1]
        )

    def own_all(k):
        all_of = (k, pl.ds(0, owners_n - 1))
        return remote(
            send1.at[all_of], recv1.at[all_of], sem_1.at[0, k], sem_1.at[1, k], "seq", across
        )

    def brief_copy(p):
        at = brief.at[half, mine_o]
        return remote(at, at, sem_b.at[0, 0], sem_b.at[1, 0], "seq", p[1])

    def brief_all():
        at = brief.at[half, pl.ds(0, owners_n - 1)]
        return remote(at, at, sem_b.at[0, 0], sem_b.at[1, 0], "seq", across)

    def brief_across():
        at = brief.at[half]
        return remote(at, at, sem_b.at[0, 1], sem_b.at[1, 1], "seq", across)

    def kz_at(tract):
        at = pl.ds(pl.multiple_of(tract * rows, rows), rows)
        return kv.at[at]

    def kz_near(i, tract, which):
        to = grp * side + half * inner_n + lax.rem(lax.rem(place, inner_n) + i, inner_n)
        at = kz_at(tract)
        return remote(at, at, sem_kz.at[0, which], sem_kz.at[1, which], "seq", to)

    def kz_near_all(which):
        at = kv.at[pl.ds(0, (inner_n - 1) * rows)]
        return remote(at, at, sem_kz.at[0, which], sem_kz.at[1, which], "seq", across)

    def kz_far(tract):
        at = kz_at(tract)
        return remote(at, at, sem_kz.at[0, 1], sem_kz.at[1, 1], "seq", across)

    for load in loads[2:4]:
        load.wait()
    kz_far(me).start()
    for i in range(1, inner_n):
        kz_near(i, me, 0).start()
    each_peer(lambda p: brief_copy(p).start())

    tail_w = jnp.where(seg_col == last_seg, jnp.exp(cs_t[rows - 1 : rows, :] - cs_t), 0.0)
    tail_two = split_two(tail_w)
    for load in loads[4:6]:
        load.wait()
    b_t = b_ref[...].astype(F32).T.astype(BF16)
    for at in range(0, chans, 256):
        lanes = slice(at, at + 256)
        tail_x = (x_ref[:, lanes].astype(F32) * mm(tail_two, grid_two[:, lanes])).astype(BF16)
        state = mm(b_t, tail_x).astype(BF16)
        w, off = divmod(at, half_chans)
        for s in range(n):
            send1[(s % 2) * 2 + w, s // 2, :, off : off + 256] = state[s * n_rows : (s + 1) * n_rows]

    brief_all().wait_recv()
    brief_across().start()
    each_peer(lambda p: own_copy(0, p).start())
    for k in range(1, chunks):
        each_peer(lambda p: own_copy(k, p).start())
    for k in range(chunks):
        recv1[k, mine_o] = send1[k, mine_o]
    near = [brief[half, o] for o in range(owners_n)]
    links = []
    for g in range(groups):
        for i in range(1, inner_n):
            a, b = near[g * inner_n + i - 1], near[g * inner_n + i]
            links.append(jnp.where(a[1:2] == b[1:2], b[0:1], 0.0))
    if links:
        links = jnp.concatenate(links + [jnp.zeros((8 - len(links), 128), F32)], axis=0)
        links = expand(links[:, 0:heads], grid)
    kz_far(me).wait_recv()
    for i in range(1, inner_n):
        kz_near(i, across, 2).start()

    def sum_copy(k):
        return remote(
            sums.at[k],
            others.at[k, pl.ds(1, groups)],
            sem_p.at[0, k],
            sem_p.at[1, k],
            "seq",
            across,
        )

    def own_lanes(k):
        return slice((k % 2) * half_chans, (k % 2 + 1) * half_chans)

    def kx_copy(to_grp, src_grp):
        at = pl.ds(pl.multiple_of(src_grp * span, span), span)
        to = to_grp * side + place
        return remote(
            kv.at[at], kv.at[at], sem_kx.at[0, to_grp], sem_kx.at[1, src_grp], "seq", to
        )

    def kx_start():
        if inner_n > 1:
            kz_near_all(0).wait_recv()
            kz_near_all(2).wait_recv()
        for g in range(1, groups):

            @pl.when(grp < g)
            def _():
                kx_copy(g, grp).start()

    for k in range(chunks):
        if k == 0:
            kx_start()
        own_all(k).wait_recv()
        for g in range(groups):
            total = recv1[k, g * inner_n].astype(F32)
            for i in range(1, inner_n):
                at = g * (inner_n - 1) + i - 1
                keep = links[at : at + 1, own_lanes(k)]
                total = total * keep + recv1[k, g * inner_n + i].astype(F32)
            sums[k, g] = total.astype(BF16)
        sum_copy(k).start()

    loads[6].wait()
    owners = own_ref[...]
    for w in range(2):
        for o in range(n_pool):
            page = jnp.zeros((page_rows, HEAD_DIM), F32)
            for g in range(n_pool):
                at = pl.ds(pl.multiple_of(mine + g * page_rows, 16), page_rows)
                part = kv[at, w * HEAD_DIM : (w + 1) * HEAD_DIM].astype(F32)
                page = jnp.where(owners[:, g : g + 1] == o, part, page)
            pages[o, w] = page.astype(BF16)

    def page_copy(k, w):
        to = lax.rem(my_pool + k, n_pool)
        dst = (ok_out, ov_out)[w].at[0, my_pool]
        return remote(pages.at[to, w], dst, sem_pool.at[0, 0], sem_pool.at[1, 0], "pool", to)

    def page_all():
        at = pages.at[pl.ds(0, n_pool - 1)]
        to = lax.rem(my_pool + 1, n_pool)
        return remote(at, at, sem_pool.at[0, 0], sem_pool.at[1, 0], "pool", to)

    def last_copy(k):
        to = lax.rem(my_pool + k, n_pool)
        return remote(
            st_send.at[to], st_out.at[my_pool], sem_pool.at[0, 1], sem_pool.at[1, 1], "pool", to
        )

    def last_all():
        at = pl.ds(0, n_pool - 1)
        to = lax.rem(my_pool + 1, n_pool)
        return remote(
            st_send.at[at], st_out.at[at], sem_pool.at[0, 1], sem_pool.at[1, 1], "pool", to
        )

    for k in range(1, n_pool):
        for w in range(2):
            page_copy(k, w).start()
    stores = [
        pltpu.make_async_copy(pages.at[my_pool, 0], ok_out.at[0, my_pool], sem_out.at[0]),
        pltpu.make_async_copy(pages.at[my_pool, 1], ov_out.at[0, my_pool], sem_out.at[1]),
        pltpu.make_async_copy(st_send.at[my_pool], st_out.at[my_pool], sem_out.at[2]),
        pltpu.make_async_copy(att_v, att_out.at[0], sem_out.at[3]),
    ]
    stores[0].start()
    stores[1].start()

    brief_across().wait_recv()
    order = [
        brief[(c % side) // inner_n, (c // side) * inner_n + c % inner_n] for c in range(n)
    ]
    line = []
    for c in range(n):
        last = order[c][1:2]
        before = order[c - 1][1:2] if c else jnp.full((1, 128), -1.0, F32)
        line.append(jnp.where(last == before, order[c][0:1], 0.0))
    run = [
        [math.prod(line[g * side + h * inner_n + i] for i in range(inner_n)) for g in range(groups)]
        for h in range(2)
    ]
    table = [jnp.where(half == 0, run[1][max(g - 1, 0)], run[0][g]) for g in range(groups)]
    for g in range(groups):
        for i in range(inner_n):
            a, b = line[g * side + i], line[g * side + inner_n + i]
            table.append(jnp.where(half == 0, a, b))
    table.append(run[1][groups - 1])
    end_at = len(table) - 1
    table = jnp.concatenate(table + [jnp.zeros((16 - len(table), 128), F32)], axis=0)
    factor[...] = expand(table[:, 0:heads], grid)

    others[:, 0] = jnp.zeros_like(others[:, 0])

    def back_copy(k, p):
        return remote(
            send2.at[k, p[0]], recv2.at[k, mine_o], sem_2.at[0, k], sem_2.at[1, k], "seq", p[1]
        )

    def back_all(k):
        all_of = (k, pl.ds(0, owners_n - 1))
        return remote(
            send2.at[all_of], recv2.at[all_of], sem_2.at[0, k], sem_2.at[1, k], "seq", across
        )

    def fin_copy(k, p):
        return remote(
            fin_send.at[k, p[0]], fin_recv.at[k, mine_o], sem_f.at[0, k], sem_f.at[1, k], "seq", p[1]
        )

    def fin_all(k):
        at = (k, pl.ds(0, owners_n - 1))
        return remote(
            fin_send.at[at], fin_recv.at[at], sem_f.at[0, k], sem_f.at[1, k], "seq", across
        )

    def scan(k):
        lanes = own_lanes(k)
        sum_copy(k).wait_recv()
        carry = jnp.zeros((n_rows, half_chans), F32)
        for g in range(groups):
            carry = carry * factor[g : g + 1, lanes] + others[k, g + half].astype(F32)
            for i in range(inner_n):
                o = g * inner_n + i
                send2[k, o] = carry.astype(BF16)
                at = groups + o
                carry = carry * factor[at : at + 1, lanes] + recv1[k, o].astype(F32)
        each_peer(lambda p: back_copy(k, p).start())
        recv2[k, mine_o] = send2[k, mine_o]

        end = carry * factor[end_at : end_at + 1, lanes] + others[k, groups].astype(F32)
        last = jnp.where(half == 0, end, carry)
        count = tiles // 2
        stacked = jnp.concatenate([last[:, t * 128 : (t + 1) * 128] for t in range(count)], axis=0)
        fin_t[...] = stacked.T
        to_lanes = slice((k % 2) * count * n_rows, (k % 2 + 1) * count * n_rows)
        for o in range(owners_n):
            first = (o // inner_n) * side + o % inner_n
            for w in range(2):
                a = w * HEAD_P + first * p_rows
                b = a + inner_n * p_rows
                part = jnp.where(half == 0, fin_t[a : a + p_rows, :], fin_t[b : b + p_rows, :])
                fin_send[k // 2, o, w * p_rows : (w + 1) * p_rows, to_lanes] = part
        if k % 2:
            each_peer(lambda p: fin_copy(k // 2, p).start())
            fin_recv[k // 2, mine_o] = fin_send[k // 2, mine_o]

    scan(0)

    for load in loads[7:]:
        load.wait()
    edge_0 = sum(o[2:3] for o in order)
    edge_1 = edge_0 + sum(o[3:4] for o in order)
    prev = jnp.maximum(me - 1, 0)
    prev_o = (prev // side) * inner_n + lax.rem(prev, inner_n)
    prev_last = brief[lax.rem(prev, side) // inner_n, prev_o][1:2, 0:1]
    prev_last = jnp.where(me == 0, -1.0, prev_last)
    enter_two = split_two(jnp.where(seg_col == prev_last, jnp.exp(cs_t), 0.0))
    skip_x = expand(jnp.broadcast_to(skip_ref[...], (8, heads)), grid)[0:1]
    inner = mm(c_ref[...], b_t)
    inner = jnp.where((col_i <= row_i) & (seg_col == seg_row), inner, 0.0)
    first_half = lax.broadcasted_iota(jnp.int32, (rows, 128), 1) < HEAD_P

    def within(pair):
        lanes = slice(pair * 128, pair * 128 + 128)
        x_pair = x_ref[:, lanes]
        y = []
        for h in (2 * pair, 2 * pair + 1):
            gap = jnp.minimum(cs_t[:, h : h + 1] - cs[h : h + 1, :], 0.0)
            y.append(mm((inner * jnp.exp(gap)).astype(BF16), x_pair))
        mix0[:, lanes] = jnp.where(first_half, y[0], y[1]) + skip_x[:, lanes] * x_pair.astype(F32)
        gate = z_ref[:, lanes].astype(F32)
        silu_z[:, lanes] = gate / (1.0 + jnp.exp(-gate))
        enter_x[:, lanes] = mm(enter_two, grid_two[:, lanes])

    for pair in range(heads // 2):
        within(pair)

    scan(1)

    lane = lax.broadcasted_iota(jnp.int32, (rows, HEAD_DIM), 1).astype(F32)
    q_doc = jnp.where(lane == seg_col, 1.0, 0.0).astype(BF16)
    for a in range(q_heads):
        qa[a * rows : (a + 1) * rows, HEAD_DIM : 2 * HEAD_DIM] = q_doc

    scale = HEAD_DIM ** (-0.5) * LOG2E
    key_lane = lax.broadcasted_iota(jnp.int32, (HEAD_DIM, span), 1)
    doc_row = lax.broadcasted_iota(jnp.int32, (HEAD_DIM, span), 0)
    causal_key = lax.broadcasted_iota(jnp.int32, (rows, span), 1)
    causal_row = lax.broadcasted_iota(jnp.int32, (rows, span), 0)
    edges = [jnp.concatenate([e] * (span // 128), axis=1) for e in (edge_0, edge_1)]

    def attend(g, first):
        at = pl.ds(pl.multiple_of(g * span, span), span)
        key_pos = (key_lane + g * span).astype(F32)
        doc = jnp.where(key_pos >= edges[0], 1, 0) + jnp.where(key_pos >= edges[1], 1, 0)
        k_doc = jnp.where((doc != doc_row) & (doc_row < 3), FAR, 0.0).astype(BF16)
        k_t = kv[at, 0:HEAD_DIM].astype(F32).T.astype(BF16)
        keys = jnp.concatenate([k_t, k_doc], axis=0)
        for a in range(q_heads):
            own = slice(a * rows, (a + 1) * rows)
            s = mm(qa[own, :], keys)
            if first:
                s = jnp.where(causal_key + g * span <= causal_row + me * rows, s, FAR)
            score[own, :] = s
            top = functools.reduce(jnp.maximum, [s[:, i : i + 128] for i in range(0, span, 128)])
            if not first:
                top = jnp.maximum(top, run_max[own])
            top = jnp.broadcast_to(jnp.max(top, axis=1, keepdims=True), (rows, 128))
            if not first:
                shrink = jnp.exp2((run_max[own] - top) * scale)
                run_sum[own] = run_sum[own] * shrink
                run_out[own] = run_out[own] * shrink
            run_max[own] = top
        values = kv[at, HEAD_DIM : 2 * HEAD_DIM]
        for a in range(q_heads):
            own = slice(a * rows, (a + 1) * rows)
            top = run_max[own]
            total = None if first else run_sum[own]
            weights = []
            for i in range(0, span, 128):
                e = jnp.exp2((score[own, i : i + 128] - top) * scale)
                total = e if total is None else total + e
                weights.append(e.astype(BF16))
            out = mm(jnp.concatenate(weights, axis=1), values)
            run_sum[own] = total
            run_out[own] = out if first else run_out[own] + out

    attend(grp, True)

    def attend_earlier(g):
        kx_copy(g, g).wait_recv()
        attend(g, False)

    def attend_rest(i, u):
        attend_earlier(grp - 1 - i)
        return u

    scan(2)
    scan(3)
    lax.fori_loop(0, grp, attend_rest, 0)
    for a in range(q_heads):
        own = slice(a * rows, (a + 1) * rows)
        total = jnp.sum(run_sum[own], axis=1, keepdims=True)
        att_v[:, a * HEAD_DIM : (a + 1) * HEAD_DIM] = (run_out[own] / total).astype(BF16)
    stores[3].start()


    for k in range(2):
        fin_all(k).wait_recv()
    last = [
        jnp.concatenate(
            [fin_recv[s % 2, s // 2, :, t * n_rows : (t + 1) * n_rows] for s in range(n)], axis=1
        )
        for t in range(tiles)
    ]
    per = tiles // n_pool
    for o in range(n_pool):
        for t in range(per):
            part = jnp.zeros_like(last[0])
            for g in range(n_pool):
                part = jnp.where(owners[:, g : g + 1] == o, last[g * per + t], part)
            for w in range(2):
                st_send[o, 2 * t + w] = part[w * p_rows : (w + 1) * p_rows]
    for k in range(1, n_pool):
        last_copy(k).start()
    stores[2].start()

    for k in range(chunks):
        own_all(k).wait_send()
        sum_copy(k).wait_send()
        back_all(k).wait_send()
    brief_all().wait_send()
    brief_across().wait_send()
    for k in range(2):
        fin_all(k).wait_send()
    kz_far(me).wait_send()
    if inner_n > 1:
        kz_near_all(0).wait_send()
        kz_near_all(2).wait_send()
    for g in range(1, groups):

        @pl.when(grp < g)
        def _():
            kx_copy(g, grp).wait_send()

    if n_pool > 1:
        page_all().wait()

    for k in range(chunks):
        back_all(k).wait_recv()
    c_all = c_ref[...]
    square = jnp.zeros((rows, 128), F32)
    for at in range(0, chans, 256):
        lanes = slice(at, at + 256)
        w, off = divmod(at, half_chans)
        entered = jnp.concatenate(
            [recv2[(s % 2) * 2 + w, s // 2, :, off : off + 256] for s in range(n)], axis=0
        )
        y = mm(c_all, entered)
        mixed = (mix0[:, lanes] + y * enter_x[:, lanes]).astype(BF16).astype(F32)
        gated = mixed * silu_z[:, lanes]
        mix0[:, lanes] = gated
        square = square + gated[:, 0:128] * gated[:, 0:128] + gated[:, 128:] * gated[:, 128:]
    mean = jnp.sum(square, axis=1, keepdims=True) * (1.0 / chans)
    norm = lax.rsqrt(mean + NORM_EPS)
    part = chans // 4
    for at in range(0, chans, 256):
        lanes = slice(at, at + 256)
        mix_v[:, lanes] = (mix0[:, lanes] * norm * gain_ref[:, lanes]).astype(BF16)
        if (at + 256) % part == 0:
            done = pl.ds(at + 256 - part, part)
            store = pltpu.make_async_copy(
                mix_v.at[:, done], mix_out.at[0, :, done], sem_out.at[4 + at // part]
            )
            store.start()
            stores.append(store)
    if n_pool > 1:
        last_all().wait()
    for store in stores:
        store.wait()


def store(*refs):
    count = (len(refs) - 2) // 3
    sem_in, sem_out = refs[-2:]
    through = refs[2 * count : 3 * count]
    loads = [pltpu.make_async_copy(refs[i], through[i], sem_in.at[i]) for i in range(count)]
    saves = [
        pltpu.make_async_copy(through[i], refs[count + i], sem_out.at[i]) for i in range(count)
    ]
    for load in loads:
        load.start()
    for load, save in zip(loads, saves):
        load.wait()
        save.start()
    for save in saves:
        save.wait()


def local(n, n_pool, *args):
    (x, z, b, c, ld, skip, gain, seg, q, k, v, owner) = args
    rows, chans = x.shape[1:]
    heads = ld.shape[1]
    q_heads = q.shape[2] // HEAD_DIM
    p_rows = HEAD_P // n
    n_rows = STATE // n
    side = math.isqrt(n)
    groups = n // side
    owners_n = n // 2
    grp_heads = heads // n_pool
    page_rows = rows // n_pool
    tiles = chans // 128
    hbm = pl.BlockSpec(memory_space=pltpu.HBM)
    pages = (n_pool, page_rows, HEAD_DIM)
    states = (n_pool, grp_heads, p_rows, STATE)
    part = (4, owners_n, n_rows, chans // 2)
    dma = pltpu.SemaphoreType.DMA
    out = pl.pallas_call(
        functools.partial(kernel, n, n_pool),
        out_shape=(
            jax.ShapeDtypeStruct(x.shape, BF16),
            jax.ShapeDtypeStruct(q.shape, BF16),
            jax.ShapeDtypeStruct(states, F32),
            jax.ShapeDtypeStruct((1,) + pages, BF16),
            jax.ShapeDtypeStruct((1,) + pages, BF16),
        ),
        in_specs=[hbm] * 12,
        out_specs=[hbm] * 5,
        scratch_shapes=[
            pltpu.VMEM((rows, chans), BF16),
            pltpu.VMEM((rows, q_heads * HEAD_DIM), BF16),
            pltpu.VMEM((rows, chans), BF16),
            pltpu.VMEM((rows, chans), BF16),
            pltpu.VMEM((rows, STATE), BF16),
            pltpu.VMEM((rows, STATE), BF16),
            pltpu.VMEM((heads, rows), F32),
            pltpu.VMEM((1, heads), F32),
            pltpu.VMEM((1, chans), F32),
            pltpu.VMEM((1, rows), jnp.int32),
            pltpu.VMEM(owner.shape, jnp.int32),
            pltpu.VMEM((q_heads * rows, 2 * HEAD_DIM), BF16),
            pltpu.VMEM((n * rows, 2 * HEAD_DIM), BF16),
            pltpu.VMEM(part, BF16),
            pltpu.VMEM(part, BF16),
            pltpu.VMEM((4, groups, n_rows, chans // 2), BF16),
            pltpu.VMEM((4, groups + 1, n_rows, chans // 2), BF16),
            pltpu.VMEM(part, BF16),
            pltpu.VMEM(part, BF16),
            pltpu.VMEM((2, owners_n, 8, 128), F32),
            pltpu.VMEM((16, chans), F32),
            pltpu.VMEM((q_heads * rows, side * rows), F32),
            pltpu.VMEM((q_heads * rows, 128), F32),
            pltpu.VMEM((q_heads * rows, 128), F32),
            pltpu.VMEM((q_heads * rows, HEAD_DIM), F32),
            pltpu.VMEM((rows, chans), F32),
            pltpu.VMEM((rows, chans), F32),
            pltpu.VMEM((rows, chans), F32),
            pltpu.VMEM((n_pool, 2, page_rows, HEAD_DIM), BF16),
            pltpu.VMEM((128, tiles // 2 * n_rows), F32),
            pltpu.VMEM((2, owners_n, 2 * p_rows, tiles * n_rows), F32),
            pltpu.VMEM((2, owners_n, 2 * p_rows, tiles * n_rows), F32),
            pltpu.VMEM(states, F32),
            dma((11 + q_heads,)),
            dma((8,)),
            dma((2, 2)),
            dma((2, 4)),
            dma((2, 4)),
            dma((2, 4)),
            dma((2, 2)),
            dma((2, 3)),
            dma((2, 4)),
            dma((2, 2)),
        ],
        compiler_params=pltpu.CompilerParams(
            collective_id=0, has_side_effects=True, vmem_limit_bytes=60 * 1024 * 1024
        ),
    )(x, z, b, c, ld, skip.reshape(1, -1), gain.reshape(1, -1), seg, q, k, v, owner)
    out = pl.pallas_call(
        store,
        out_shape=tuple(jax.ShapeDtypeStruct(o.shape, o.dtype) for o in out),
        in_specs=[hbm] * 5,
        out_specs=[hbm] * 5,
        scratch_shapes=[pltpu.VMEM(o.shape, o.dtype) for o in out] + [dma((5,)), dma((5,))],
        compiler_params=pltpu.CompilerParams(vmem_limit_bytes=60 * 1024 * 1024),
    )(*out)
    mixer, attended, owned, keys, values = out
    return mixer, attended, owned[None], keys, values


def solution(mesh):
    return jax.shard_map(
        functools.partial(local, mesh.shape["seq"], mesh.shape["pool"]),
        mesh=mesh,
        in_specs=(
            P("pool", "seq", "head"),
            P("pool", "seq", "head"),
            P("pool", "seq", "head"),
            P("pool", "seq", "head"),
            P("pool", "head", "seq"),
            P("head"),
            P("head"),
            P("pool", "seq"),
            P("pool", "seq", "head"),
            P("pool", "seq", "head"),
            P("pool", "seq", "head"),
            P("pool", "head"),
        ),
        out_specs=(
            P("pool", "seq", "head"),
            P("pool", "seq", "head"),
            P("pool", None, "head", "seq", None),
            P("pool", None, "seq", "head"),
            P("pool", None, "seq", "head"),
        ),
        check_vma=False,
    )
```

time: 115 us -> 69.1 us (0.60)
  the two profiles are of different devices: /device:TPU:6 before, /device:TPU:132 now
where the time goes in v3:
time: 69.1 us; the launch traced here: 68.9 us
  Pallas kernels  68.3 us (99%)
    pallas_call x1, Pallas kernels, local(): pl.pallas_call(functools.partial(kernel, n, n_pool), out_shape=(jax.Shape...  66 us
    pallas_call x1, Pallas kernels, local(): pl.pallas_call(store, out_shape=tuple((jax.ShapeDtypeStruct(o.shape, o.dt...  2.29 us

profile of v3, /device:TPU:132, one launch (start us, length us, event | category | flops | bytes accessed | tf_op | source)
XLA Modules:
  0.0 68.9 jit_solution(13070566925201515250)
XLA Ops:
  0.6 66.0 %shard_map.155 = (bf16[1,192,2048]{2,1,0:T(8,128)(2,1)}, bf16[1,192,1024]{2,1,0:T(8,128)(2,1)}, f32[4,8,4,256]{3,2,1,0:T(4,128)}, bf16[1,4,48,128]{3,2,1,0:T(8,128)(2,1)}, bf16[1,4,48,128]{3,2,1,0:T(8,128)(2,1)}) custom-call(bf16[1,192,2048]{2,1,0:T(8,128)(2,1)} %x_hbm.1, bf16[1,192,2048]{2,1,0:T(8,128)(2,1)} %z_hbm.1, bf16[1,192,256]{2,1,0:T(8,128)(2,1)} %b_hbm.1, ...), custom_call_target="tpu_custom_call" | custom-call | tf_op jit(solution)/shard_map/pallas_call | solution.py:674
  66.7 2.3 %shard_map.156 = (bf16[1,192,2048]{2,1,0:T(8,128)(2,1)}, bf16[1,192,1024]{2,1,0:T(8,128)(2,1)}, f32[4,8,4,256]{3,2,1,0:T(4,128)}, bf16[1,4,48,128]{3,2,1,0:T(8,128)(2,1)}, bf16[1,4,48,128]{3,2,1,0:T(8,128)(2,1)}) custom-call(bf16[1,192,2048]{2,1,0:T(8,128)(2,1)} %get-tuple-element.15.refs_0_, bf16[1,192,1024]{2,1,0:T(8,128)(2,1)} %get-tuple-element.16.refs_1_, ...), custom_call_target="tpu_custom_call" | custom-call | tf_op jit(solution)/shard_map/pallas_call | solution.py:734

commit v4 on v3

--- a/solution.py
+++ b/solution.py
@@ -265,7 +265,7 @@
     for load in loads[4:6]:
         load.wait()
     b_t = b_ref[...].astype(F32).T.astype(BF16)
-    for at in range(0, chans, 256):
+    def make_state(at):
         lanes = slice(at, at + 256)
         tail_x = (x_ref[:, lanes].astype(F32) * mm(tail_two, grid_two[:, lanes])).astype(BF16)
         state = mm(b_t, tail_x).astype(BF16)
@@ -273,9 +273,13 @@
         for s in range(n):
             send1[(s % 2) * 2 + w, s // 2, :, off : off + 256] = state[s * n_rows : (s + 1) * n_rows]
 
+    for at in range(0, half_chans, 256):
+        make_state(at)
     brief_all().wait_recv()
     brief_across().start()
     each_peer(lambda p: own_copy(0, p).start())
+    for at in range(half_chans, chans, 256):
+        make_state(at)
     for k in range(1, chunks):
         each_peer(lambda p: own_copy(k, p).start())
     for k in range(chunks):
@@ -581,34 +585,14 @@
         last_copy(k).start()
     stores[2].start()
 
-    for k in range(chunks):
-        own_all(k).wait_send()
-        sum_copy(k).wait_send()
-        back_all(k).wait_send()
-    brief_all().wait_send()
-    brief_across().wait_send()
-    for k in range(2):
-        fin_all(k).wait_send()
-    kz_far(me).wait_send()
-    if inner_n > 1:
-        kz_near_all(0).wait_send()
-        kz_near_all(2).wait_send()
-    for g in range(1, groups):
-
-        @pl.when(grp < g)
-        def _():
-            kx_copy(g, grp).wait_send()
-
-    if n_pool > 1:
-        page_all().wait()
-
-    for k in range(chunks):
-        back_all(k).wait_recv()
     c_all = c_ref[...]
     square = jnp.zeros((rows, 128), F32)
     for at in range(0, chans, 256):
         lanes = slice(at, at + 256)
         w, off = divmod(at, half_chans)
+        if off == 0:
+            back_all(w).wait_recv()
+            back_all(w + 2).wait_recv()
         entered = jnp.concatenate(
             [recv2[(s % 2) * 2 + w, s // 2, :, off : off + 256] for s in range(n)], axis=0
         )
@@ -630,6 +614,27 @@
             )
             store.start()
             stores.append(store)
+    for k in range(chunks):
+        own_all(k).wait_send()
+        sum_copy(k).wait_send()
+        back_all(k).wait_send()
+    brief_all().wait_send()
+    brief_across().wait_send()
+    for k in range(2):
+        fin_all(k).wait_send()
+    kz_far(me).wait_send()
+    if inner_n > 1:
+        kz_near_all(0).wait_send()
+        kz_near_all(2).wait_send()
+    for g in range(1, groups):
+
+        @pl.when(grp < g)
+        def _():
+            kx_copy(g, grp).wait_send()
+
+    if n_pool > 1:
+        page_all().wait()
+
     if n_pool > 1:
         last_all().wait()
     for store in stores:
@@ -640,9 +645,16 @@
     count = (len(refs) - 2) // 3
     sem_in, sem_out = refs[-2:]
     through = refs[2 * count : 3 * count]
-    loads = [pltpu.make_async_copy(refs[i], through[i], sem_in.at[i]) for i in range(count)]
+    rows = refs[0].shape[1] // 4
+    pieces = [(0, (0, pl.ds(i * rows, rows))) for i in range(4)]
+    pieces += [(i, (slice(None),)) for i in range(1, count)]
+    loads = [
+        pltpu.make_async_copy(refs[i].at[at], through[i].at[at], sem_in.at[j])
+        for j, (i, at) in enumerate(pieces)
+    ]
     saves = [
-        pltpu.make_async_copy(through[i], refs[count + i], sem_out.at[i]) for i in range(count)
+        pltpu.make_async_copy(through[i].at[at], refs[count + i].at[at], sem_out.at[j])
+        for j, (i, at) in enumerate(pieces)
     ]
     for load in loads:
         load.start()
@@ -736,7 +748,7 @@
         out_shape=tuple(jax.ShapeDtypeStruct(o.shape, o.dtype) for o in out),
         in_specs=[hbm] * 5,
         out_specs=[hbm] * 5,
-        scratch_shapes=[pltpu.VMEM(o.shape, o.dtype) for o in out] + [dma((5,)), dma((5,))],
+        scratch_shapes=[pltpu.VMEM(o.shape, o.dtype) for o in out] + [dma((8,)), dma((8,))],
         compiler_params=pltpu.CompilerParams(vmem_limit_bytes=60 * 1024 * 1024),
     )(*out)
     mixer, attended, owned, keys, values = out

time: 69.1 us -> 69.1 us (level)
  no operation moved by 1% of the time
where the time goes in v4:
time: 69.1 us; the launch traced here: 69 us
  Pallas kernels  68.3 us (99%)
    pallas_call x1, Pallas kernels, local(): pl.pallas_call(functools.partial(kernel, n, n_pool), out_shape=(jax.Shape...  66 us
    pallas_call x1, Pallas kernels, local(): pl.pallas_call(store, out_shape=tuple((jax.ShapeDtypeStruct(o.shape, o.dt...  2.3 us

profile of v4, /device:TPU:132, one launch (start us, length us, event | category | flops | bytes accessed | tf_op | source)
XLA Modules:
  0.0 69.0 jit_solution(7727556640619367881)
XLA Ops:
  0.6 66.0 %shard_map.155 = (bf16[1,192,2048]{2,1,0:T(8,128)(2,1)}, bf16[1,192,1024]{2,1,0:T(8,128)(2,1)}, f32[4,8,4,256]{3,2,1,0:T(4,128)}, bf16[1,4,48,128]{3,2,1,0:T(8,128)(2,1)}, bf16[1,4,48,128]{3,2,1,0:T(8,128)(2,1)}) custom-call(bf16[1,192,2048]{2,1,0:T(8,128)(2,1)} %x_hbm.1, bf16[1,192,2048]{2,1,0:T(8,128)(2,1)} %z_hbm.1, bf16[1,192,256]{2,1,0:T(8,128)(2,1)} %b_hbm.1, ...), custom_call_target="tpu_custom_call" | custom-call | tf_op jit(solution)/shard_map/pallas_call | solution.py:686
  66.7 2.3 %shard_map.156 = (bf16[1,192,2048]{2,1,0:T(8,128)(2,1)}, bf16[1,192,1024]{2,1,0:T(8,128)(2,1)}, f32[4,8,4,256]{3,2,1,0:T(4,128)}, bf16[1,4,48,128]{3,2,1,0:T(8,128)(2,1)}, bf16[1,4,48,128]{3,2,1,0:T(8,128)(2,1)}) custom-call(bf16[1,192,2048]{2,1,0:T(8,128)(2,1)} %get-tuple-element.15.refs_0_, bf16[1,192,1024]{2,1,0:T(8,128)(2,1)} %get-tuple-element.16.refs_1_, ...), custom_call_target="tpu_custom_call" | custom-call | tf_op jit(solution)/shard_map/pallas_call | solution.py:746
